TPU v7x, 128 devices: a whole 4x4x4 slice. The times are simulated.
128 devices in a mesh: sec: 16 (over x, y), sub: 8 (over z, core).
Axes of the slice: x: 4, y: 4, z: 4, core: 2. Of those that a mesh axis runs over, the one named last changes fastest.
Arguments:
- charges: bfloat16 [32768, 128], P(('sec', 'sub')), may hold values from -6 to 6
- positions: float32 [3, 32768, 128], P(None, ('sec', 'sub')), may hold values from 0 to 1
- p2m: bfloat16 [128, 128], replicated, may hold values from -0.5 to 0.5
- m2m: bfloat16 [8, 128, 128], replicated, may hold values from -0.1875 to 0.1875
- m2l: bfloat16 [316, 128, 128], replicated, may hold values from -0.0390625 to 0.0390625
- l2l: bfloat16 [8, 128, 128], replicated, may hold values from -0.5 to 0.5
- l2p: bfloat16 [128, 128], replicated, may hold values from -0.5 to 0.5
- send_rows: int32 [128, 128, 32], P(('sec', 'sub')), may hold values from 0 to 255
- send_counts: int32 [128, 128], P(('sec', 'sub')), may hold values from 1 to 32, as said below
- leaf_list: int32 [32768, 189], P(('sec', 'sub')), may hold values from 0 to 4351, as said below
- leaf_types: int32 [32768, 189], P(('sec', 'sub')), may hold values from 0 to 315, as said below
- parent_list: int32 [4096, 189], P(('sec', 'sub')), may hold values from 0 to 4095
- parent_types: int32 [4096, 189], P(('sec', 'sub')), may hold values from 0 to 315, as said below
- near_list: int32 [16, 32768, 128], P(None, ('sec', 'sub')), may hold values from 0 to 1024
Outputs:
- potential: float32 [32768, 128], P(('sec', 'sub'))
Inputs may be any that keep to these rules, and one draw needn't show every extreme that they name: `send_counts`: the live slots of every block are at least one; in every draw some owner receives full blocks of 32 from every source. `leaf_list`: every entry names a live slot of a received block or one of the owner's own leaves. `leaf_types`: the 189 entries of one row are distinct translation vectors. `parent_types`: the 189 entries of one row are distinct translation vectors.
All inputs are finite; a program needn't handle non-finite values.
Results may differ from a plain program's by a relative error of at most 0.006.
Values may be sent and summed in bfloat16 or wider, within the bound.
A program may use at most 128 MiB of HBM per device.

v0:
```python
import jax
import jax.numpy as jnp
from jax import lax
from jax.sharding import PartitionSpec as P

RIM = 512


softening = 0.0025


def passed_along(block, axis, distance):
    devices = range(lax.axis_size(axis))
    route = [(i - distance, i) for i in devices if i - distance in devices]
    return lax.ppermute(block, axis, route)


def apply_kinds(sources, kinds, m2l):
    kind_count = m2l.shape[0]
    onehot = (kinds[..., None] == jnp.arange(kind_count, dtype=jnp.int32)).astype(jnp.bfloat16)
    grouped = jnp.einsum(
        "bkt,bkp->btp", onehot, sources, preferred_element_type=jnp.float32
    ).astype(jnp.bfloat16)
    return jnp.einsum("btp,tpq->bq", grouped, m2l, preferred_element_type=jnp.float32)


def local(
    charges,
    positions,
    p2m,
    m2m,
    m2l,
    l2l,
    l2p,
    send_rows,
    send_counts,
    leaf_list,
    leaf_types,
    parent_list,
    parent_types,
    near_list,
):
    leaf_dev, panels = charges.shape
    coeffs = p2m.shape[1]
    capacity = send_rows.shape[2]
    devices = lax.axis_size(("sec", "sub"))
    parent_dev = leaf_dev // 8
    multipole = jnp.dot(charges, p2m, preferred_element_type=jnp.float32).astype(jnp.bfloat16)
    children = multipole.reshape(parent_dev, 8, coeffs)
    parent_multipole = jnp.einsum(
        "cop,opq->cq", children, m2m, preferred_element_type=jnp.float32
    ).astype(jnp.bfloat16)
    keep = jnp.arange(capacity, dtype=jnp.int32)[None, :] < send_counts[0][:, None]
    outgoing = jnp.where(keep[..., None], multipole[send_rows[0]], jnp.zeros((), jnp.bfloat16))
    arrived = lax.all_to_all(outgoing, ("sec", "sub"), split_axis=0, concat_axis=0, tiled=True)
    table = jnp.concatenate([arrived.reshape(devices * capacity, coeffs), multipole], 0)
    everyone = lax.all_gather(parent_multipole, ("sec", "sub"), axis=0, tiled=True)
    picked = everyone[parent_list]
    parent_local = apply_kinds(picked, parent_types, m2l).astype(jnp.bfloat16)
    block = min(leaf_dev, 128)
    lists_b = leaf_list.reshape(leaf_dev // block, block, leaf_list.shape[1])
    kinds_b = leaf_types.reshape(leaf_dev // block, block, leaf_types.shape[1])

    def one_block(pair):
        return apply_kinds(table[pair[0]], pair[1], m2l)

    leaf_local = lax.map(one_block, (lists_b, kinds_b)).reshape(leaf_dev, coeffs)
    downward = jnp.einsum(
        "cp,opq->coq", parent_local, l2l, preferred_element_type=jnp.float32
    ).reshape(leaf_dev, coeffs)
    leaf_total = (leaf_local + downward).astype(jnp.bfloat16)
    far = jnp.dot(leaf_total, l2p, preferred_element_type=jnp.float32)
    packed = jnp.concatenate(
        [
            positions.reshape(3, leaf_dev * panels),
            charges.astype(jnp.float32).reshape(1, leaf_dev * panels),
        ],
        0,
    )
    lower_rim = passed_along(packed[:, leaf_dev * panels - RIM :], ("sec", "sub"), 1)
    upper_rim = passed_along(packed[:, :RIM], ("sec", "sub"), -1)
    window = jnp.concatenate([lower_rim, packed, upper_rim], 1)
    span = panels + 2 * RIM
    group = min(leaf_dev, 16)
    columns = jnp.arange(span, dtype=jnp.int32)
    within = jnp.arange(panels, dtype=jnp.int32)

    def near_group(index):
        first = index * group
        starts = (first + jnp.arange(group, dtype=jnp.int32)) * panels

        def cut(begin):
            return lax.dynamic_slice_in_dim(window, begin, span, 1)

        frames = jax.vmap(cut)(starts)
        centres = lax.dynamic_slice_in_dim(positions, first, group, 1)
        offsets = lax.dynamic_slice_in_dim(near_list, first, group, 1)
        targets = offsets + within[None, None, :]
        counts = jnp.zeros((group, panels, span), jnp.float32)
        for entry in range(offsets.shape[0]):
            counts = counts + (targets[entry][..., None] == columns).astype(jnp.float32)
        distance = jnp.zeros((group, panels, span), jnp.float32)
        for axis_c in range(3):
            delta = centres[axis_c][:, :, None] - frames[:, axis_c][:, None, :]
            distance = distance + delta * delta
        kernel = frames[:, 3][:, None, :] / jnp.sqrt(distance + softening)
        return jnp.sum(counts * kernel, axis=-1)

    near = (
        lax.map(near_group, jnp.arange(leaf_dev // group, dtype=jnp.int32)).reshape(
            leaf_dev, panels
        )
        / near_list.shape[0]
    )
    return far + near


def solution(mesh):
    in_specs = (
        P(("sec", "sub"), None),
        P(None, ("sec", "sub"), None),
        P(),
        P(),
        P(),
        P(),
        P(),
        P(("sec", "sub"), None, None),
        P(("sec", "sub"), None),
        P(("sec", "sub"), None),
        P(("sec", "sub"), None),
        P(("sec", "sub"), None),
        P(("sec", "sub"), None),
        P(None, ("sec", "sub"), None),
    )
    out_specs = P(("sec", "sub"), None)
    return jax.shard_map(local, mesh=mesh, in_specs=in_specs, out_specs=out_specs, check_vma=False)
```

profile of v0, /device:TPU:1, one launch (start us, length us, event | category | flops | bytes accessed | tf_op | source)
XLA Modules:
  0.0 1156.2 jit_solution(88137982405173317)
XLA Ops:
  46.1 830.2 %while.28 = (s32[]{:T(128)}, f32[16,16,128]{2,1,0:T(8,128)S(1)}, s32[16]{0:T(128)S(1)}, s32[16,256,128]{2,1,0:T(8,128)}, f32[4,33792]{1,0:T(4,128)S(1)}, /*index...) while((s32[]{:T(128)}, f32[16,16,128]{2,1,0:T(8,128)S(1)}, ...), condition=%wide.region_4.5_spmd.clone.clone, body=%wide.region_2.4_spmd.clone.clone.sunk | while | flops 139229280 | bytes 2265724 | solution.py:110
  49.1 22.6 %while.29 = (s32[]{:T(128)}, f32[4,33792]{1,0:T(4,128)S(1)}, s32[16,2]{0,1:T(2,128)S(1)}, f32[16,4,1152]{2,1,0:T(4,128)S(1)}, s32[]{:T(128)}) while((s32[]{:T(128)}, f32[4,33792]{1,0:T(4,128)S(1)}, s32[16,2]{0,1:T(2,128)S(1)}, f32[16,4,1152]{2,1,0:T(4,128)S(1)}, s32[]{:T(128)}) %tuple.88), condition=%wide.while_cond, body=%wide.while_body.sunk | while | flops 2 | bytes 36961 | solution.py:93
  72.0 26.0 %multiply_reduce_fusion.2 = f32[16,128]{1,0:T(8,128)S(1)} fusion(f32[16,1152]{1,0:T(8,128)S(1)} %get-tuple-element.388, f32[16,128]{1,0:T(8,128)S(1)} %get-tuple-element.389, f32[16,1152]{1,0:T(8,128)S(1)} %get-tuple-element.390, f32[16,128]{1,0:T(8,128)S(1)} %get-tuple-element.391, f32[16,1152]{1,0:T(8,128)S(1)} %get-tuple-element.394, ...), kind=kLoop, calls=%fused_computation.33.clone.1 | loop fusion | flops 139196416 | bytes 458752 | tf_op jit(solution)/shard_map/while/body/eval_jaxpr/reduce_sum | solution.py:107
  101.0 22.6 %while.29 = (s32[]{:T(128)}, f32[4,33792]{1,0:T(4,128)S(1)}, s32[16,2]{0,1:T(2,128)S(1)}, f32[16,4,1152]{2,1,0:T(4,128)S(1)}, s32[]{:T(128)}) while((s32[]{:T(128)}, f32[4,33792]{1,0:T(4,128)S(1)}, s32[16,2]{0,1:T(2,128)S(1)}, f32[16,4,1152]{2,1,0:T(4,128)S(1)}, s32[]{:T(128)}) %tuple.88), condition=%wide.while_cond, body=%wide.while_body.sunk | while | flops 2 | bytes 36961 | solution.py:93
  123.9 26.0 %multiply_reduce_fusion.2 = f32[16,128]{1,0:T(8,128)S(1)} fusion(f32[16,1152]{1,0:T(8,128)S(1)} %get-tuple-element.388, f32[16,128]{1,0:T(8,128)S(1)} %get-tuple-element.389, f32[16,1152]{1,0:T(8,128)S(1)} %get-tuple-element.390, f32[16,128]{1,0:T(8,128)S(1)} %get-tuple-element.391, f32[16,1152]{1,0:T(8,128)S(1)} %get-tuple-element.394, ...), kind=kLoop, calls=%fused_computation.33.clone.1 | loop fusion | flops 139196416 | bytes 458752 | tf_op jit(solution)/shard_map/while/body/eval_jaxpr/reduce_sum | solution.py:107
  152.9 22.6 %while.29 = (s32[]{:T(128)}, f32[4,33792]{1,0:T(4,128)S(1)}, s32[16,2]{0,1:T(2,128)S(1)}, f32[16,4,1152]{2,1,0:T(4,128)S(1)}, s32[]{:T(128)}) while((s32[]{:T(128)}, f32[4,33792]{1,0:T(4,128)S(1)}, s32[16,2]{0,1:T(2,128)S(1)}, f32[16,4,1152]{2,1,0:T(4,128)S(1)}, s32[]{:T(128)}) %tuple.88), condition=%wide.while_cond, body=%wide.while_body.sunk | while | flops 2 | bytes 36961 | solution.py:93
  175.7 26.0 %multiply_reduce_fusion.2 = f32[16,128]{1,0:T(8,128)S(1)} fusion(f32[16,1152]{1,0:T(8,128)S(1)} %get-tuple-element.388, f32[16,128]{1,0:T(8,128)S(1)} %get-tuple-element.389, f32[16,1152]{1,0:T(8,128)S(1)} %get-tuple-element.390, f32[16,128]{1,0:T(8,128)S(1)} %get-tuple-element.391, f32[16,1152]{1,0:T(8,128)S(1)} %get-tuple-element.394, ...), kind=kLoop, calls=%fused_computation.33.clone.1 | loop fusion | flops 139196416 | bytes 458752 | tf_op jit(solution)/shard_map/while/body/eval_jaxpr/reduce_sum | solution.py:107
  204.7 22.6 %while.29 = (s32[]{:T(128)}, f32[4,33792]{1,0:T(4,128)S(1)}, s32[16,2]{0,1:T(2,128)S(1)}, f32[16,4,1152]{2,1,0:T(4,128)S(1)}, s32[]{:T(128)}) while((s32[]{:T(128)}, f32[4,33792]{1,0:T(4,128)S(1)}, s32[16,2]{0,1:T(2,128)S(1)}, f32[16,4,1152]{2,1,0:T(4,128)S(1)}, s32[]{:T(128)}) %tuple.88), condition=%wide.while_cond, body=%wide.while_body.sunk | while | flops 2 | bytes 36961 | solution.py:93
  227.6 26.0 %multiply_reduce_fusion.2 = f32[16,128]{1,0:T(8,128)S(1)} fusion(f32[16,1152]{1,0:T(8,128)S(1)} %get-tuple-element.388, f32[16,128]{1,0:T(8,128)S(1)} %get-tuple-element.389, f32[16,1152]{1,0:T(8,128)S(1)} %get-tuple-element.390, f32[16,128]{1,0:T(8,128)S(1)} %get-tuple-element.391, f32[16,1152]{1,0:T(8,128)S(1)} %get-tuple-element.394, ...), kind=kLoop, calls=%fused_computation.33.clone.1 | loop fusion | flops 139196416 | bytes 458752 | tf_op jit(solution)/shard_map/while/body/eval_jaxpr/reduce_sum | solution.py:107
  256.6 22.6 %while.29 = (s32[]{:T(128)}, f32[4,33792]{1,0:T(4,128)S(1)}, s32[16,2]{0,1:T(2,128)S(1)}, f32[16,4,1152]{2,1,0:T(4,128)S(1)}, s32[]{:T(128)}) while((s32[]{:T(128)}, f32[4,33792]{1,0:T(4,128)S(1)}, s32[16,2]{0,1:T(2,128)S(1)}, f32[16,4,1152]{2,1,0:T(4,128)S(1)}, s32[]{:T(128)}) %tuple.88), condition=%wide.while_cond, body=%wide.while_body.sunk | while | flops 2 | bytes 36961 | solution.py:93
  279.5 26.0 %multiply_reduce_fusion.2 = f32[16,128]{1,0:T(8,128)S(1)} fusion(f32[16,1152]{1,0:T(8,128)S(1)} %get-tuple-element.388, f32[16,128]{1,0:T(8,128)S(1)} %get-tuple-element.389, f32[16,1152]{1,0:T(8,128)S(1)} %get-tuple-element.390, f32[16,128]{1,0:T(8,128)S(1)} %get-tuple-element.391, f32[16,1152]{1,0:T(8,128)S(1)} %get-tuple-element.394, ...), kind=kLoop, calls=%fused_computation.33.clone.1 | loop fusion | flops 139196416 | bytes 458752 | tf_op jit(solution)/shard_map/while/body/eval_jaxpr/reduce_sum | solution.py:107
  308.5 22.6 %while.29 = (s32[]{:T(128)}, f32[4,33792]{1,0:T(4,128)S(1)}, s32[16,2]{0,1:T(2,128)S(1)}, f32[16,4,1152]{2,1,0:T(4,128)S(1)}, s32[]{:T(128)}) while((s32[]{:T(128)}, f32[4,33792]{1,0:T(4,128)S(1)}, s32[16,2]{0,1:T(2,128)S(1)}, f32[16,4,1152]{2,1,0:T(4,128)S(1)}, s32[]{:T(128)}) %tuple.88), condition=%wide.while_cond, body=%wide.while_body.sunk | while | flops 2 | bytes 36961 | solution.py:93
  331.4 26.0 %multiply_reduce_fusion.2 = f32[16,128]{1,0:T(8,128)S(1)} fusion(f32[16,1152]{1,0:T(8,128)S(1)} %get-tuple-element.388, f32[16,128]{1,0:T(8,128)S(1)} %get-tuple-element.389, f32[16,1152]{1,0:T(8,128)S(1)} %get-tuple-element.390, f32[16,128]{1,0:T(8,128)S(1)} %get-tuple-element.391, f32[16,1152]{1,0:T(8,128)S(1)} %get-tuple-element.394, ...), kind=kLoop, calls=%fused_computation.33.clone.1 | loop fusion | flops 139196416 | bytes 458752 | tf_op jit(solution)/shard_map/while/body/eval_jaxpr/reduce_sum | solution.py:107
  360.4 22.6 %while.29 = (s32[]{:T(128)}, f32[4,33792]{1,0:T(4,128)S(1)}, s32[16,2]{0,1:T(2,128)S(1)}, f32[16,4,1152]{2,1,0:T(4,128)S(1)}, s32[]{:T(128)}) while((s32[]{:T(128)}, f32[4,33792]{1,0:T(4,128)S(1)}, s32[16,2]{0,1:T(2,128)S(1)}, f32[16,4,1152]{2,1,0:T(4,128)S(1)}, s32[]{:T(128)}) %tuple.88), condition=%wide.while_cond, body=%wide.while_body.sunk | while | flops 2 | bytes 36961 | solution.py:93
  383.3 26.0 %multiply_reduce_fusion.2 = f32[16,128]{1,0:T(8,128)S(1)} fusion(f32[16,1152]{1,0:T(8,128)S(1)} %get-tuple-element.388, f32[16,128]{1,0:T(8,128)S(1)} %get-tuple-element.389, f32[16,1152]{1,0:T(8,128)S(1)} %get-tuple-element.390, f32[16,128]{1,0:T(8,128)S(1)} %get-tuple-element.391, f32[16,1152]{1,0:T(8,128)S(1)} %get-tuple-element.394, ...), kind=kLoop, calls=%fused_computation.33.clone.1 | loop fusion | flops 139196416 | bytes 458752 | tf_op jit(solution)/shard_map/while/body/eval_jaxpr/reduce_sum | solution.py:107
  412.3 22.6 %while.29 = (s32[]{:T(128)}, f32[4,33792]{1,0:T(4,128)S(1)}, s32[16,2]{0,1:T(2,128)S(1)}, f32[16,4,1152]{2,1,0:T(4,128)S(1)}, s32[]{:T(128)}) while((s32[]{:T(128)}, f32[4,33792]{1,0:T(4,128)S(1)}, s32[16,2]{0,1:T(2,128)S(1)}, f32[16,4,1152]{2,1,0:T(4,128)S(1)}, s32[]{:T(128)}) %tuple.88), condition=%wide.while_cond, body=%wide.while_body.sunk | while | flops 2 | bytes 36961 | solution.py:93
  435.2 26.0 %multiply_reduce_fusion.2 = f32[16,128]{1,0:T(8,128)S(1)} fusion(f32[16,1152]{1,0:T(8,128)S(1)} %get-tuple-element.388, f32[16,128]{1,0:T(8,128)S(1)} %get-tuple-element.389, f32[16,1152]{1,0:T(8,128)S(1)} %get-tuple-element.390, f32[16,128]{1,0:T(8,128)S(1)} %get-tuple-element.391, f32[16,1152]{1,0:T(8,128)S(1)} %get-tuple-element.394, ...), kind=kLoop, calls=%fused_computation.33.clone.1 | loop fusion | flops 139196416 | bytes 458752 | tf_op jit(solution)/shard_map/while/body/eval_jaxpr/reduce_sum | solution.py:107
  464.2 22.6 %while.29 = (s32[]{:T(128)}, f32[4,33792]{1,0:T(4,128)S(1)}, s32[16,2]{0,1:T(2,128)S(1)}, f32[16,4,1152]{2,1,0:T(4,128)S(1)}, s32[]{:T(128)}) while((s32[]{:T(128)}, f32[4,33792]{1,0:T(4,128)S(1)}, s32[16,2]{0,1:T(2,128)S(1)}, f32[16,4,1152]{2,1,0:T(4,128)S(1)}, s32[]{:T(128)}) %tuple.88), condition=%wide.while_cond, body=%wide.while_body.sunk | while | flops 2 | bytes 36961 | solution.py:93
  487.1 26.0 %multiply_reduce_fusion.2 = f32[16,128]{1,0:T(8,128)S(1)} fusion(f32[16,1152]{1,0:T(8,128)S(1)} %get-tuple-element.388, f32[16,128]{1,0:T(8,128)S(1)} %get-tuple-element.389, f32[16,1152]{1,0:T(8,128)S(1)} %get-tuple-element.390, f32[16,128]{1,0:T(8,128)S(1)} %get-tuple-element.391, f32[16,1152]{1,0:T(8,128)S(1)} %get-tuple-element.394, ...), kind=kLoop, calls=%fused_computation.33.clone.1 | loop fusion | flops 139196416 | bytes 458752 | tf_op jit(solution)/shard_map/while/body/eval_jaxpr/reduce_sum | solution.py:107
  516.1 22.6 %while.29 = (s32[]{:T(128)}, f32[4,33792]{1,0:T(4,128)S(1)}, s32[16,2]{0,1:T(2,128)S(1)}, f32[16,4,1152]{2,1,0:T(4,128)S(1)}, s32[]{:T(128)}) while((s32[]{:T(128)}, f32[4,33792]{1,0:T(4,128)S(1)}, s32[16,2]{0,1:T(2,128)S(1)}, f32[16,4,1152]{2,1,0:T(4,128)S(1)}, s32[]{:T(128)}) %tuple.88), condition=%wide.while_cond, body=%wide.while_body.sunk | while | flops 2 | bytes 36961 | solution.py:93
  539.0 26.0 %multiply_reduce_fusion.2 = f32[16,128]{1,0:T(8,128)S(1)} fusion(f32[16,1152]{1,0:T(8,128)S(1)} %get-tuple-element.388, f32[16,128]{1,0:T(8,128)S(1)} %get-tuple-element.389, f32[16,1152]{1,0:T(8,128)S(1)} %get-tuple-element.390, f32[16,128]{1,0:T(8,128)S(1)} %get-tuple-element.391, f32[16,1152]{1,0:T(8,128)S(1)} %get-tuple-element.394, ...), kind=kLoop, calls=%fused_computation.33.clone.1 | loop fusion | flops 139196416 | bytes 458752 | tf_op jit(solution)/shard_map/while/body/eval_jaxpr/reduce_sum | solution.py:107
  590.9 26.0 %multiply_reduce_fusion.2 = f32[16,128]{1,0:T(8,128)S(1)} fusion(f32[16,1152]{1,0:T(8,128)S(1)} %get-tuple-element.388, f32[16,128]{1,0:T(8,128)S(1)} %get-tuple-element.389, f32[16,1152]{1,0:T(8,128)S(1)} %get-tuple-element.390, f32[16,128]{1,0:T(8,128)S(1)} %get-tuple-element.391, f32[16,1152]{1,0:T(8,128)S(1)} %get-tuple-element.394, ...), kind=kLoop, calls=%fused_computation.33.clone.1 | loop fusion | flops 139196416 | bytes 458752 | tf_op jit(solution)/shard_map/while/body/eval_jaxpr/reduce_sum | solution.py:107
  619.9 22.6 %while.29 = (s32[]{:T(128)}, f32[4,33792]{1,0:T(4,128)S(1)}, s32[16,2]{0,1:T(2,128)S(1)}, f32[16,4,1152]{2,1,0:T(4,128)S(1)}, s32[]{:T(128)}) while((s32[]{:T(128)}, f32[4,33792]{1,0:T(4,128)S(1)}, s32[16,2]{0,1:T(2,128)S(1)}, f32[16,4,1152]{2,1,0:T(4,128)S(1)}, s32[]{:T(128)}) %tuple.88), condition=%wide.while_cond, body=%wide.while_body.sunk | while | flops 2 | bytes 36961 | solution.py:93
  642.8 26.0 %multiply_reduce_fusion.2 = f32[16,128]{1,0:T(8,128)S(1)} fusion(f32[16,1152]{1,0:T(8,128)S(1)} %get-tuple-element.388, f32[16,128]{1,0:T(8,128)S(1)} %get-tuple-element.389, f32[16,1152]{1,0:T(8,128)S(1)} %get-tuple-element.390, f32[16,128]{1,0:T(8,128)S(1)} %get-tuple-element.391, f32[16,1152]{1,0:T(8,128)S(1)} %get-tuple-element.394, ...), kind=kLoop, calls=%fused_computation.33.clone.1 | loop fusion | flops 139196416 | bytes 458752 | tf_op jit(solution)/shard_map/while/body/eval_jaxpr/reduce_sum | solution.py:107
  694.6 26.0 %multiply_reduce_fusion.2 = f32[16,128]{1,0:T(8,128)S(1)} fusion(f32[16,1152]{1,0:T(8,128)S(1)} %get-tuple-element.388, f32[16,128]{1,0:T(8,128)S(1)} %get-tuple-element.389, f32[16,1152]{1,0:T(8,128)S(1)} %get-tuple-element.390, f32[16,128]{1,0:T(8,128)S(1)} %get-tuple-element.391, f32[16,1152]{1,0:T(8,128)S(1)} %get-tuple-element.394, ...), kind=kLoop, calls=%fused_computation.33.clone.1 | loop fusion | flops 139196416 | bytes 458752 | tf_op jit(solution)/shard_map/while/body/eval_jaxpr/reduce_sum | solution.py:107
  746.5 26.0 %multiply_reduce_fusion.2 = f32[16,128]{1,0:T(8,128)S(1)} fusion(f32[16,1152]{1,0:T(8,128)S(1)} %get-tuple-element.388, f32[16,128]{1,0:T(8,128)S(1)} %get-tuple-element.389, f32[16,1152]{1,0:T(8,128)S(1)} %get-tuple-element.390, f32[16,128]{1,0:T(8,128)S(1)} %get-tuple-element.391, f32[16,1152]{1,0:T(8,128)S(1)} %get-tuple-element.394, ...), kind=kLoop, calls=%fused_computation.33.clone.1 | loop fusion | flops 139196416 | bytes 458752 | tf_op jit(solution)/shard_map/while/body/eval_jaxpr/reduce_sum | solution.py:107
  775.5 22.6 %while.29 = (s32[]{:T(128)}, f32[4,33792]{1,0:T(4,128)S(1)}, s32[16,2]{0,1:T(2,128)S(1)}, f32[16,4,1152]{2,1,0:T(4,128)S(1)}, s32[]{:T(128)}) while((s32[]{:T(128)}, f32[4,33792]{1,0:T(4,128)S(1)}, s32[16,2]{0,1:T(2,128)S(1)}, f32[16,4,1152]{2,1,0:T(4,128)S(1)}, s32[]{:T(128)}) %tuple.88), condition=%wide.while_cond, body=%wide.while_body.sunk | while | flops 2 | bytes 36961 | solution.py:93
  798.4 26.0 %multiply_reduce_fusion.2 = f32[16,128]{1,0:T(8,128)S(1)} fusion(f32[16,1152]{1,0:T(8,128)S(1)} %get-tuple-element.388, f32[16,128]{1,0:T(8,128)S(1)} %get-tuple-element.389, f32[16,1152]{1,0:T(8,128)S(1)} %get-tuple-element.390, f32[16,128]{1,0:T(8,128)S(1)} %get-tuple-element.391, f32[16,1152]{1,0:T(8,128)S(1)} %get-tuple-element.394, ...), kind=kLoop, calls=%fused_computation.33.clone.1 | loop fusion | flops 139196416 | bytes 458752 | tf_op jit(solution)/shard_map/while/body/eval_jaxpr/reduce_sum | solution.py:107
  850.3 26.0 %multiply_reduce_fusion.2 = f32[16,128]{1,0:T(8,128)S(1)} fusion(f32[16,1152]{1,0:T(8,128)S(1)} %get-tuple-element.388, f32[16,128]{1,0:T(8,128)S(1)} %get-tuple-element.389, f32[16,1152]{1,0:T(8,128)S(1)} %get-tuple-element.390, f32[16,128]{1,0:T(8,128)S(1)} %get-tuple-element.391, f32[16,1152]{1,0:T(8,128)S(1)} %get-tuple-element.394, ...), kind=kLoop, calls=%fused_computation.33.clone.1 | loop fusion | flops 139196416 | bytes 458752 | tf_op jit(solution)/shard_map/while/body/eval_jaxpr/reduce_sum | solution.py:107
  877.1 239.7 %while.26 = (s32[]{:T(128)}, f32[2,128,128]{2,1,0:T(8,128)S(1)}, s32[2,128,189]{1,0,2:T(2,128)S(1)}, s32[2,128,189]{2,1,0:T(8,128)S(1)}, bf16[4352,128]{1,0:T(8,...) while((s32[]{:T(128)}, f32[2,128,128]{2,1,0:T(8,128)S(1)}, s32[2,128,189]{1,0,2:T(2,128)S(1)}, ...), condition=%wide.region_1.2_spmd, body=%wide.region_0.1_spmd.sunk | while | flops 3295355392 | bytes 93836880 | solution.py:67
  877.7 49.4 %gather_fusion = bf16[24192,128]{1,0:T(8,128)(2,1)} fusion(bf16[4352,128]{1,0:T(8,128)(2,1)S(1)} %get-tuple-element.490, s32[24576]{0:T(1024)S(1)} %pad_clamp_fusion.3), kind=kCustom, calls=%fused_computation.clone.1 | custom fusion | bytes 12483072 | tf_op jit(solution)/shard_map/while/body/eval_jaxpr/gather | solution.py:65
  997.3 49.4 %gather_fusion = bf16[24192,128]{1,0:T(8,128)(2,1)} fusion(bf16[4352,128]{1,0:T(8,128)(2,1)S(1)} %get-tuple-element.490, s32[24576]{0:T(1024)S(1)} %pad_clamp_fusion.3), kind=kCustom, calls=%fused_computation.clone.1 | custom fusion | bytes 12483072 | tf_op jit(solution)/shard_map/while/body/eval_jaxpr/gather | solution.py:65
  (1024 shorter events, 705.7 us)
Async XLA Ops:
  6.5 1135.6 %copy-start = (bf16[8,128,128]{2,1,0:T(8,128)(2,1)S(1)}, bf16[8,128,128]{2,1,0:T(8,128)(2,1)}, u32[]{:S(2)}) copy-start(bf16[8,128,128]{2,1,0:T(8,128)(2,1)} %param.23) | copy-start | bytes 786436
  6.5 36.7 %copy-start.2 = (bf16[8,128,128]{2,1,0:T(8,128)(2,1)S(1)}, bf16[8,128,128]{2,1,0:T(8,128)(2,1)}, u32[]{:S(2)}) copy-start(bf16[8,128,128]{2,1,0:T(8,128)(2,1)} %param.21) | copy-start | bytes 786436
  6.5 37.5 %copy-start.6 = (s32[32,189]{1,0:T(8,128)S(1)}, s32[32,189]{1,0:T(8,128)}, u32[]{:S(2)}) copy-start(s32[32,189]{1,0:T(8,128)} %param.29) | copy-start | bytes 72580
  6.5 38.3 %copy-start.3 = (s32[256,189]{0,1:T(8,128)S(1)}, s32[256,189]{0,1:T(8,128)}, u32[]{:S(2)}) copy-start(s32[256,189]{0,1:T(8,128)} %param.27) | copy-start | bytes 580612
  6.5 38.5 %copy-start.4 = (s32[256,189]{0,1:T(8,128)S(1)}, s32[256,189]{0,1:T(8,128)}, u32[]{:S(2)}) copy-start(s32[256,189]{0,1:T(8,128)} %param.28) | copy-start | bytes 580612
  9.4 35.8 %collective-permute-start = (f32[4,512]{1,0:T(4,128)}, f32[4,512]{1,0:T(4,128)S(1)}, u32[]{:S(2)}, u32[]{:S(2)}) collective-permute-start(f32[4,512]{1,0:T(4,128)} %get-tuple-element.252), channel_id=1, source_target_pairs={{0,1},{1,2},{2,3},{3,4},{4,5},{5,6},{6,7},{7,8},{8,9},{9,10},{10,1... | collective-permute-start | bytes 24584 | tf_op jit(solution)/shard_map/ppermute | solution.py:15
  14.3 30.8 %collective-permute-start.1 = (f32[4,512]{1,0:T(4,128)S(1)}, f32[4,512]{1,0:T(4,128)}, u32[]{:S(2)}, u32[]{:S(2)}) collective-permute-start(f32[4,512]{1,0:T(4,128)S(1)} %get-tuple-element.253), channel_id=1, source_target_pairs={{1,0},{2,1},{3,2},{4,3},{5,4},{6,5},{7,6},{8,7},{9,8},{10,9},{11,1... | collective-permute-start | bytes 24584 | tf_op jit(solution)/shard_map/ppermute | solution.py:15
  33.0 844.0 %all-to-all-start = ((bf16[128,32,128]{2,1,0:T(8,128)(2,1)}), bf16[128,32,128]{2,1,0:T(8,128)(2,1)S(1)}, u32[]{:S(2)}, u32[]{:S(2)}) async-start(bf16[128,32,128]{2,1,0:T(8,128)(2,1)} %broadcast_select_fusion), calls=%async_computation | async-start | bytes 2097152 | tf_op jit(solution)/shard_map/all_to_all | solution.py:55
  43.2 1073.6 %all-gather.2.cloned.1.call-start = ((), (), s32[]{:S(2)}) async-start(), calls=%async_computation.1 | async-start | bytes 1056768 | tf_op jit(solution)/shard_map/all_gather | solution.py:57
  877.1 239.8 %copy-start.5 = (s32[6144]{0:T(1024)S(1)}, s32[6144]{0:T(1024)}, u32[]{:S(2)}) copy-start(s32[6144]{0:T(1024)} %pad_clamp_fusion.1) | copy-start | bytes 73732
  1116.8 19.6 %copy-start.8 = (s32[32,189]{1,0:T(8,128)S(1)}, s32[32,189]{1,0:T(8,128)}, u32[]{:S(2)}) copy-start(s32[32,189]{1,0:T(8,128)} %param.30) | copy-start | bytes 72580
  1136.4 12.1 %copy-start.1 = (f32[16,16,128]{2,1,0:T(8,128)S(1)}, f32[16,16,128]{2,1,0:T(8,128)}, u32[]{:S(2)}) copy-start(f32[16,16,128]{2,1,0:T(8,128)} %broadcast_multiply_fusion) | copy-start | bytes 393220
  1136.4 12.1 %copy-start.7 = (bf16[128,128]{1,0:T(8,128)(2,1)S(1)}, bf16[128,128]{1,0:T(8,128)(2,1)}, u32[]{:S(2)}) copy-start(bf16[128,128]{1,0:T(8,128)(2,1)} %param.24) | copy-start | bytes 98308
Sparse Core Ops, SparseCore 0:
  46.9 65.4 all-gather.1
where the time goes:
time: 1160 us
  local copies, waits for them, and re-layouts  581 us (50%)
  other arithmetic  452 us (39%)
  matrix products  79.1 us (7%)
  starting transfers between devices  17.1 us (1%)
  between operations  13.6 us (1%)
  loops' own time  12.7 us (1%)
    reduce_sum x16, other arithmetic, near_group(): return jnp.sum(counts * kernel, axis=-1)  416 us
    gather x768, local copies, waits for them, and re-layouts  362 us
    gather x4, local copies, waits for them, and re-layouts, one_block(): return apply_kinds(table[pair[0]], pair[1], m2l)  116 us
    eq x2, local copies, waits for them, and re-layouts, apply_kinds(): kinds[..., None] == jnp.arange(kind_count, dtype=jnp.int32)  43.9 us
    dot_general x3, matrix products, apply_kinds(): jnp.einsum('bkt,bkp->btp', onehot, sources, preferred_element_type=jnp.fl...  43.8 us
    dot_general x2, matrix products, apply_kinds(): jnp.einsum('btp,tpq->bq', grouped, m2l, preferred_element_type=jnp.float32)  26.6 us
  transfers between devices with their start and end apart: 4, of which 0 were waited for; matrix products, arithmetic and copies ran while one was open for 93% of the time, Pallas kernels for 0%

commit v1 on v0

v1 whole, which is shorter than its diff:
```python
import functools

import jax
import jax.numpy as jnp
from jax import lax
from jax.experimental import pallas as pl
from jax.experimental.pallas import tpu as pltpu
from jax.sharding import PartitionSpec as P

RIM = 512
SOFT = 0.0025
BOTH = ("sec", "sub")
F32 = jnp.float32
BF16 = jnp.bfloat16
I32 = jnp.int32
SMEM = pl.BlockSpec(memory_space=pltpu.SMEM)
VMEM = pl.BlockSpec(memory_space=pltpu.VMEM)
ANY = pl.BlockSpec(memory_space=pl.ANY)


def passed_along(block, axis, distance):
    devices = range(lax.axis_size(axis))
    route = [(i - distance, i) for i in devices if i - distance in devices]
    return lax.ppermute(block, axis, route)


def prepare_kernel(rows_ref, charges_ref, p2m_ref, m2m_ref, mult_ref, parent_ref, out_ref, wide, block):
    mult = jnp.dot(charges_ref[...], p2m_ref[...], preferred_element_type=F32).astype(BF16)
    mult_ref[...] = mult
    wide[...] = mult.astype(F32)
    parents = parent_ref.shape[0]
    total = jnp.zeros(parent_ref.shape, F32)
    for octant in range(8):
        child = wide[pl.ds(octant, parents, stride=8), :].astype(BF16)
        total = total + jnp.dot(child, m2m_ref[octant], preferred_element_type=F32)
    parent_ref[...] = total.astype(BF16)
    step = block.shape[0]

    def some(g, carry):
        rows = rows_ref.at[pl.ds(g * step, step)]
        for u in range(step):
            block[pl.ds(u, 1), :] = wide[pl.ds(rows[u], 1), :]
        out_ref[pl.ds(pl.multiple_of(g * step, step), step), :] = block[...].astype(BF16)
        return carry

    lax.fori_loop(0, out_ref.shape[0] // step, some, 0)


def prepare(rows, charges, p2m, m2m):
    leaf_dev, coeffs = charges.shape[0], p2m.shape[1]
    return pl.pallas_call(
        prepare_kernel,
        out_shape=(
            jax.ShapeDtypeStruct((leaf_dev, coeffs), BF16),
            jax.ShapeDtypeStruct((leaf_dev // 8, coeffs), BF16),
            jax.ShapeDtypeStruct((rows.shape[0], coeffs), BF16),
        ),
        in_specs=[SMEM, VMEM, VMEM, VMEM],
        out_specs=(VMEM, VMEM, VMEM),
        scratch_shapes=[pltpu.VMEM((leaf_dev, coeffs), F32), pltpu.VMEM((128, coeffs), F32)],
        compiler_params=pltpu.CompilerParams(vmem_limit_bytes=32 << 20),
        name="prepare",
    )(rows, charges, p2m, m2m)


Z_SCALE = 2.0**-10


def near_kernel(pos_ref, charge_ref, low_ref, high_ref, list_ref, near_ref, xy, zq):
    leaf_dev, panels = near_ref.shape
    rim = low_ref.shape[1]

    def store(x, y, z, q, first, count):
        whole_x = jnp.round(x * 65535.0).astype(I32) - 32768
        whole_y = jnp.round(y * 65535.0).astype(I32)
        xy[pl.ds(first, count), :] = whole_x * 65536 + whole_y
        zq[pl.ds(first, count), :] = q * (1.0 + (z - 0.5) * Z_SCALE)

    store(low_ref[0], low_ref[1], low_ref[2], low_ref[3], 0, rim)
    store(pos_ref[0], pos_ref[1], pos_ref[2], charge_ref[...].astype(F32), rim, leaf_dev)
    store(high_ref[0], high_ref[1], high_ref[2], high_ref[3], rim + leaf_dev, rim)
    lane = lax.broadcasted_iota(I32, (8, panels), 1)
    shifts = 2 * rim + 1

    def group(g, carry):
        base = pl.multiple_of(g * 8, 8)
        x = pos_ref[0, pl.ds(base, 8), :]
        y = pos_ref[1, pl.ds(base, 8), :]
        z = pos_ref[2, pl.ds(base, 8), :]
        total = jnp.zeros((8, panels), F32)
        for n in range(list_ref.shape[0]):
            target = list_ref[n, pl.ds(base, 8), :] + lane
            which = target >> 7
            place = target & (panels - 1)
            word = jnp.zeros((8, panels), I32)
            weight = jnp.zeros((8, panels), F32)
            for q in range(shifts):
                at = which == q
                word = jnp.where(at, jnp.take_along_axis(xy[pl.ds(base + q, 8), :], place, axis=1), word)
                weight = jnp.where(at, jnp.take_along_axis(zq[pl.ds(base + q, 8), :], place, axis=1), weight)
            strength = weight.astype(BF16).astype(F32)
            safe = jnp.where(strength == 0.0, 1.0, strength)
            far_z = (weight - strength) / safe * (1.0 / Z_SCALE) + 0.5
            far_x = ((word >> 16) + 32768).astype(F32) * (1.0 / 65535.0)
            far_y = (word & 65535).astype(F32) * (1.0 / 65535.0)
            dx, dy, dz = x - far_x, y - far_y, z - far_z
            total = total + strength * lax.rsqrt(dx * dx + dy * dy + dz * dz + SOFT)
        near_ref[pl.ds(base, 8), :] = total * (1.0 / list_ref.shape[0])
        return carry

    lax.fori_loop(0, leaf_dev // 8, group, 0)


def near_field(positions, charges, low, high, near_list):
    leaf_dev, panels = charges.shape
    full = leaf_dev + 2 * low.shape[1]
    return pl.pallas_call(
        near_kernel,
        out_shape=jax.ShapeDtypeStruct((leaf_dev, panels), F32),
        in_specs=[VMEM] * 5,
        out_specs=VMEM,
        scratch_shapes=[pltpu.VMEM((full, panels), I32), pltpu.VMEM((full, panels), F32)],
        compiler_params=pltpu.CompilerParams(vmem_limit_bytes=32 << 20),
        cost_estimate=pl.CostEstimate(flops=30_000_000_00, bytes_accessed=4_000_000, transcendentals=1_000_000),
        name="near",
    )(positions, charges, low, high, near_list)


GROUP = 16
HALF = 8


def far_kernel(
    lists_hbm, types_ref, arrived_ref, own_ref, parents_ref, m2l_hbm, l2l_ref, l2p_ref, near_ref, out_ref,
    table, rows, tall, grouped, m2l, total, index_a, index_b, sems,
):
    boxes = types_ref.shape[0]
    wide = types_ref.shape[1]
    kinds, coeffs = m2l.shape[0], m2l.shape[2]
    steps = boxes // GROUP
    entries = index_a.shape[1]
    rows[...] = jnp.zeros_like(rows)

    def fetch(block, buffer, which):
        at = pl.multiple_of(block * HALF, HALF)
        return pltpu.make_async_copy(lists_hbm.at[pl.ds(at, HALF), :], buffer, sems.at[which])

    weights = pltpu.make_async_copy(m2l_hbm, m2l, sems.at[2])
    fetch(0, index_a, 0).start()
    fetch(1, index_b, 1).start()
    weights.start()
    first = 0
    for source in (arrived_ref, own_ref, parents_ref):
        count = source.shape[0]
        table[pl.ds(first, count), :] = source[...].astype(F32)
        first += count
    kind_of = lax.broadcasted_iota(I32, (tall.shape[0] // GROUP, wide), 0)

    def some(step, carry):
        for half, index in ((0, index_a), (1, index_b)):
            fetch(step * 2 + half, index, half).wait()
            for j in range(HALF):
                box = half * HALF + j
                for k in range(entries):
                    rows[pl.ds(box * wide + k, 1), :] = table[pl.ds(index[j, k], 1), :]

            @pl.when(step + 1 < steps)
            def _():
                fetch((step + 1) * 2 + half, index, half).start()

            for j in range(HALF):
                box = half * HALF + j
                kind = types_ref[pl.ds(step * GROUP + box, 1), :]
                onehot = (kind_of == kind).astype(BF16)
                picked = rows[pl.ds(box * wide, wide), :].astype(BF16)
                tall[pl.ds(box, kind_of.shape[0], stride=GROUP), :] = jnp.dot(onehot, picked, preferred_element_type=F32)
        at = pl.multiple_of(step * GROUP, GROUP)
        for t in range(kinds):
            grouped[t, pl.ds(at, GROUP), :] = tall[pl.ds(t * GROUP, GROUP), :].astype(BF16)
        return carry

    lax.fori_loop(0, steps, some, 0)
    weights.wait()
    total[...] = jnp.zeros_like(total)
    chunk = 12

    def multiply(first, count):
        left = jnp.concatenate([grouped[first + t] for t in range(count)], axis=1)
        right = m2l[pl.ds(first, count)].reshape(count * coeffs, coeffs)
        total[...] += jnp.dot(left, right, preferred_element_type=F32)

    def several(i, carry):
        multiply(i * chunk, chunk)
        return carry

    lax.fori_loop(0, kinds // chunk, several, 0)
    if kinds % chunk:
        multiply(kinds // chunk * chunk, kinds % chunk)
    leaf_dev = out_ref.shape[0]
    parents = boxes - leaf_dev
    parent_local = total[pl.ds(leaf_dev, parents), :].astype(BF16)
    for octant in range(8):
        down = jnp.dot(parent_local, l2l_ref[octant], preferred_element_type=F32)
        total[pl.ds(octant, parents, stride=8), :] += down
    leaf_total = total[pl.ds(0, leaf_dev), :].astype(BF16)
    out_ref[...] = jnp.dot(leaf_total, l2p_ref[...], preferred_element_type=F32) + near_ref[...]


def far_field(lists, types, arrived, own, parents, m2l, l2l, l2p, near):
    boxes, wide = types.shape
    kinds, coeffs = m2l.shape[0], m2l.shape[2]
    tables = arrived.shape[0] + own.shape[0] + parents.shape[0]
    kinds_up = -(-kinds // 16) * 16
    return pl.pallas_call(
        far_kernel,
        out_shape=jax.ShapeDtypeStruct(near.shape, F32),
        in_specs=[ANY, VMEM, VMEM, VMEM, VMEM, ANY, VMEM, VMEM, VMEM],
        out_specs=VMEM,
        scratch_shapes=[
            pltpu.VMEM((tables, coeffs), F32),
            pltpu.VMEM((GROUP * wide, coeffs), F32),
            pltpu.VMEM((kinds_up * GROUP, coeffs), F32),
            pltpu.VMEM((kinds, boxes, coeffs), BF16),
            pltpu.VMEM(m2l.shape, BF16),
            pltpu.VMEM((boxes, coeffs), F32),
            pltpu.SMEM((HALF, lists.shape[1]), I32),
            pltpu.SMEM((HALF, lists.shape[1]), I32),
            pltpu.SemaphoreType.DMA((3,)),
        ],
        compiler_params=pltpu.CompilerParams(vmem_limit_bytes=56 << 20),
        name="far",
    )(lists, types, arrived, own, parents, m2l, l2l, l2p, near)


def local(
    charges, positions, p2m, m2m, m2l, l2l, l2p,
    send_rows, send_counts, leaf_list, leaf_types, parent_list, parent_types, near_list,
):
    leaf_dev, panels = charges.shape
    coeffs = p2m.shape[1]
    capacity = send_rows.shape[2]
    devices = lax.axis_size(BOTH)
    rim = RIM // panels
    edge = lambda part: jnp.concatenate([positions[:, part], charges[part].astype(F32)[None]], 0)
    low = passed_along(edge(slice(leaf_dev - rim, leaf_dev)), BOTH, 1)
    high = passed_along(edge(slice(0, rim)), BOTH, -1)
    own, parent_own, outgoing = prepare(send_rows.reshape(devices * capacity), charges, p2m, m2m)
    arrived = lax.all_to_all(
        outgoing.reshape(devices, capacity, coeffs), BOTH, split_axis=0, concat_axis=0, tiled=True
    ).reshape(devices * capacity, coeffs)
    parents = lax.all_gather(lax.all_gather(parent_own, "sub", axis=0, tiled=True), "sec", axis=0, tiled=True)
    near = near_field(positions, charges, low, high, near_list)
    entries = leaf_list.shape[1]
    wide = -(-entries // 16) * 16
    pad = ((0, 0), (0, wide - entries))
    lists = jnp.concatenate([leaf_list, parent_list + (devices * capacity + leaf_dev)], 0)
    types = jnp.concatenate([leaf_types, parent_types], 0)
    types = jnp.pad(types, pad, constant_values=-1)
    return far_field(lists, types, arrived, own, parents, m2l, l2l, l2p, near)


def solution(mesh):
    along = P(BOTH, None)
    in_specs = (
        along, P(None, BOTH, None), P(), P(), P(), P(), P(),
        P(BOTH, None, None), along, along, along, along, along, P(None, BOTH, None),
    )
    return jax.shard_map(local, mesh=mesh, in_specs=in_specs, out_specs=along, check_vma=False)
```

time: 1160 us -> 161 us (0.14)
  local copies, waits for them, and re-layouts: 581 us -> 11.7 us
  other arithmetic: 452 us -> 2.99 us
  Pallas kernels: 0 us -> 94 us
  matrix products: 79.1 us -> 0 us
  blocking collectives: 0 us -> 16.3 us
  loops' own time: 12.7 us -> 0 us
    gather x775 -> x0, local copies, waits for them, and re-layouts: 509 us -> none
    reduce_sum x16 -> x0, other arithmetic: 416 us -> none  [near_group(): return jnp.sum(counts * kernel, axis=-1)]
    pallas_call x0 -> x3, Pallas kernels: none -> 94 us  [the longest x1 73.3 us: far_field(): pl.pallas_call(far_kernel, out_shape=jax.ShapeDtypeStruct(near.shape, F32...]
    dot_general x9 -> x0, matrix products: 79.1 us -> none  [the longest x3 43.8 us: apply_kinds(): jnp.einsum('bkt,bkp->btp', onehot, sources, preferred_element_type=jnp.fl...]
    eq x18 -> x0, local copies, waits for them, and re-layouts: 44.2 us -> none  [the longest x2 43.9 us: apply_kinds(): kinds[..., None] == jnp.arange(kind_count, dtype=jnp.int32)]
    all_gather x0 -> x1, blocking collectives: none -> 16.3 us  [local(): lax.all_gather(parent_own, 'sub', axis=0, tiled=True)]
    add x16 -> x1, other arithmetic: 14.8 us -> 0.76 us  [local(): parent_list + (devices * capacity + leaf_dev)]
    eq x2 -> x0, other arithmetic: 14.1 us -> none  [apply_kinds(): kinds[..., None] == jnp.arange(kind_count, dtype=jnp.int32)]
  transfers between devices with their start and end apart: 4 -> 4, of which waited for: 0 -> 1; matrix products, arithmetic and copies ran while one was open for 93% -> 4% of each run, Pallas kernels for 0% -> 9%
where the time goes in v1:
time: 161 us; the launch traced here: 160 us
  Pallas kernels  94 us (58%)
  blocking collectives  16.3 us (10%)
  starting transfers between devices  14.6 us (9%)
  between operations  13.5 us (8%)
  local copies, waits for them, and re-layouts  11.7 us (7%)
  waiting for transfers between devices  6.68 us (4%)
  other arithmetic  2.99 us (2%)
    pallas_call x1, Pallas kernels, far_field(): pl.pallas_call(far_kernel, out_shape=jax.ShapeDtypeStruct(near.shape, F32...  73.3 us
    all_gather x1, blocking collectives, local(): lax.all_gather(parent_own, 'sub', axis=0, tiled=True)  16.3 us
    pallas_call x1, Pallas kernels, near_field(): pl.pallas_call(near_kernel, out_shape=jax.ShapeDtypeStruct((leaf_dev, pan...  14.7 us
    unnamed x21, local copies, waits for them, and re-layouts  10.2 us
    all_to_all x1, starting transfers between devices, local(): lax.all_to_all(outgoing.reshape(devices, capacity, coeffs), BOTH, split_a...  9.05 us
    all_gather x1, waiting for transfers between devices, local(): lax.all_gather(lax.all_gather(parent_own, 'sub', axis=0, tiled=True), 'se...  6.66 us
    pallas_call x1, Pallas kernels, prepare(): pl.pallas_call(prepare_kernel, out_shape=(jax.ShapeDtypeStruct((leaf_dev,...  5.99 us
    ppermute x2, starting transfers between devices, passed_along(): return lax.ppermute(block, axis, route)  5.57 us
  transfers between devices with their start and end apart: 4, of which 1 were waited for; matrix products, arithmetic and copies ran while one was open for 4% of the time, Pallas kernels for 9%

profile of v1, /device:TPU:1, one launch (start us, length us, event | category | flops | bytes accessed | tf_op | source)
XLA Modules:
  0.0 159.7 jit_solution(12914901963685400428)
XLA Ops:
  6.5 0.0 all-gather.2.cloned.1.call-start
  6.5 0.8 copy.18
  7.3 0.1 reshape.9.rows_ref
  7.4 0.0 copy-start
  7.4 0.9 copy-done
  8.4 0.8 copy-done.2
  9.2 0.8 copy-done.5
  10.0 6.0 %prepare.1 = (bf16[256,128]{1,0:T(8,128)(2,1)S(1)}, bf16[32,128]{1,0:T(8,128)(2,1)S(1)}, bf16[4096,128]{1,0:T(8,128)(2,1)}) custom-call(s32[4096]{0:T(1024)S(1)} %reshape.9.rows_ref, bf16[256,128]{1,0:T(8,128)(2,1)S(1)} %copy-done.2, bf16[128,128]{1,0:T(8,128)(2,1)S(1)} %copy-done.5, bf16[8,128,128]{2,1,0:T(8,128)(2,1)S(1)} %copy-done), custom_call_target="tpu_custom_call" | custom-call | tf_op jit(solution)/shard_map/prepare/pallas_call | solution.py:51
  16.0 0.6 copy-done.4
  16.6 16.3 %all_gather.6 = bf16[256,128]{1,0:T(8,128)(2,1)} all-gather(bf16[32,128]{1,0:T(8,128)(2,1)S(1)} %get-tuple-element.10), channel_id=1, replica_groups=mesh['sec'=16,'sub'=8] {'sub'}, dimensions={0}, use_global_device_ids=true | all-gather | bytes 73728 | tf_op jit(solution)/shard_map/all_gather | solution.py:251
  32.9 0.0 all-gather.2.cloned.1.call-update
  32.9 9.0 %all-to-all-start = ((bf16[128,32,128]{2,1,0:T(8,128)(2,1)}), bf16[128,32,128]{2,1,0:T(8,128)(2,1)S(1)}, u32[]{:S(2)}, u32[]{:S(2)}) async-start(bf16[128,32,128]{2,1,0:T(8,128)(2,1)} %bitcast), calls=%async_computation | async-start | bytes 2097152 | tf_op jit(solution)/shard_map/all_to_all | solution.py:248
  42.0 0.7 fusion
  42.7 0.7 bitcast_convert_fusion
  43.4 3.6 %collective-permute-start = (f32[4,4,128]{2,1,0:T(4,128)S(1)}, f32[4,4,128]{2,1,0:T(4,128)S(1)}, u32[]{:S(2)}, u32[]{:S(2)}) collective-permute-start(f32[4,4,128]{2,1,0:T(4,128)S(1)} %pad_maximum_fusion), channel_id=1, source_target_pairs={{0,1},{1,2},{2,3},{3,4},{4,5},{5,6},{6,7},{7,8},{8,9},{9,10},{10,1... | collective-permute-start | bytes 24584 | tf_op jit(solution)/shard_map/ppermute | solution.py:24
  47.1 1.9 %collective-permute-start.1 = (f32[4,4,128]{2,1,0:T(4,128)S(1)}, f32[4,4,128]{2,1,0:T(4,128)S(1)}, u32[]{:S(2)}, u32[]{:S(2)}) collective-permute-start(f32[4,4,128]{2,1,0:T(4,128)S(1)} %pad_maximum_fusion.1), channel_id=1, source_target_pairs={{1,0},{2,1},{3,2},{4,3},{5,4},{6,5},{7,6},{8,7},{9,8},{10,9},{11,1... | collective-permute-start | bytes 24584 | tf_op jit(solution)/shard_map/ppermute | solution.py:24
  49.0 1.1 copy.16
  50.1 1.1 copy.17
  51.1 0.8 broadcast_add_fusion
  51.9 0.7 pad_add_fusion.lists_hbm
  52.6 0.8 pad_add_fusion.1
  53.4 0.7 pad.4.types_ref
  54.1 0.0 collective-permute-done.low_ref
  54.1 0.0 collective-permute-done.1.high_ref
  54.2 0.8 copy-done.3
  55.0 1.0 copy-done.6
  56.0 1.6 copy-done.7
  57.6 14.7 %near.1.near_ref = f32[256,128]{1,0:T(8,128)S(1)} custom-call(f32[3,256,128]{2,1,0:T(8,128)S(1)} %copy-done.6, bf16[256,128]{1,0:T(8,128)(2,1)S(1)} %copy-done.3, f32[4,4,128]{2,1,0:T(4,128)S(1)} %collective-permute-done.low_ref, f32[4,4,128]{2,1,0:T(4,128)S(1)} %collective-permute-done.1.high_ref, s32[16,256,128]{2,1,0:T(8,128)S(1)} %copy-done.7), custom_call_target="tpu_custom_call" | custom-call | flops 3000000000 | bytes 4000000 | tf_op jit(solution)/shard_map/near/pallas_call | solution.py:117
  72.3 0.6 copy-done.1
  73.0 0.0 all-to-all-done
  73.0 6.7 %all-gather.2.cloned.1.call-done.parents_ref = bf16[4096,128]{1,0:T(8,128)(2,1)} async-done(((bf16[256,128]{1,0:T(8,128)(2,1)}), bf16[4096,128]{1,0:T(8,128)(2,1)}) %all-gather.2.cloned.1.call-update) | async-done | bytes 1048592 | tf_op jit(solution)/shard_map/all_gather | solution.py:251
  79.6 73.3 %far.1 = f32[256,128]{1,0:T(8,128)} custom-call(s32[288,189]{1,0:T(8,128)} %pad_add_fusion.lists_hbm, s32[288,192]{1,0:T(8,128)} %pad.4.types_ref, bf16[4096,128]{1,0:T(8,128)(2,1)} %bitcast.8, bf16[256,128]{1,0:T(8,128)(2,1)} %copy-done.4, bf16[4096,128]{1,0:T(8,128)(2,1)} %all-gather.2.cloned.1.call-done.parents_ref, bf16[316,128,128]{2,1,0:T(8,128)(2,1)} %m2l_hbm.1, ...), custom_call_target="tpu_custom_call" | custom-call | tf_op jit(solution)/shard_map/far/pallas_call | solution.py:214
  (11 shorter events, 0.0 us)
Async XLA Ops:
  6.5 73.1 %all-gather.2.cloned.1.call-start = ((), (), s32[]{:S(2)}) async-start(), calls=%async_computation.1 | async-start | bytes 1114112 | tf_op jit(solution)/shard_map/all_gather | solution.py:251
  7.4 1.0 copy-start
  8.4 0.8 copy-start.2
  9.2 0.8 copy-start.5
  16.0 0.6 copy-start.4
  32.9 40.1 %all-to-all-start = ((bf16[128,32,128]{2,1,0:T(8,128)(2,1)}), bf16[128,32,128]{2,1,0:T(8,128)(2,1)S(1)}, u32[]{:S(2)}, u32[]{:S(2)}) async-start(bf16[128,32,128]{2,1,0:T(8,128)(2,1)} %bitcast), calls=%async_computation | async-start | bytes 2097152 | tf_op jit(solution)/shard_map/all_to_all | solution.py:248
  43.4 10.7 %collective-permute-start = (f32[4,4,128]{2,1,0:T(4,128)S(1)}, f32[4,4,128]{2,1,0:T(4,128)S(1)}, u32[]{:S(2)}, u32[]{:S(2)}) collective-permute-start(f32[4,4,128]{2,1,0:T(4,128)S(1)} %pad_maximum_fusion), channel_id=1, source_target_pairs={{0,1},{1,2},{2,3},{3,4},{4,5},{5,6},{6,7},{7,8},{8,9},{9,10},{10,1... | collective-permute-start | bytes 24584 | tf_op jit(solution)/shard_map/ppermute | solution.py:24
  47.1 7.1 %collective-permute-start.1 = (f32[4,4,128]{2,1,0:T(4,128)S(1)}, f32[4,4,128]{2,1,0:T(4,128)S(1)}, u32[]{:S(2)}, u32[]{:S(2)}) collective-permute-start(f32[4,4,128]{2,1,0:T(4,128)S(1)} %pad_maximum_fusion.1), channel_id=1, source_target_pairs={{1,0},{2,1},{3,2},{4,3},{5,4},{6,5},{7,6},{8,7},{9,8},{10,9},{11,1... | collective-permute-start | bytes 24584 | tf_op jit(solution)/shard_map/ppermute | solution.py:24
  54.1 0.8 copy-start.3
  55.0 1.0 copy-start.6
  56.0 1.6 copy-start.7
  72.3 0.7 copy-start.1
  73.0 6.7 %copy-start.8 = (bf16[128,32,128]{2,1,0:T(8,128)(2,1)}, bf16[128,32,128]{2,1,0:T(8,128)(2,1)S(1)}, u32[]{:S(2)}) copy-start(bf16[128,32,128]{2,1,0:T(8,128)(2,1)S(1)} %all-to-all-done) | copy-start | bytes 3145732
Sparse Core Ops, SparseCore 0:
  33.0 46.5 all-gather.1

commit v2 on v1

v2 whole, which is shorter than its diff:
```python
import functools

import jax
import jax.numpy as jnp
from jax import lax
from jax.experimental import pallas as pl
from jax.experimental.pallas import tpu as pltpu
from jax.sharding import PartitionSpec as P

RIM = 512
SOFT = 0.0025
BOTH = ("sec", "sub")
F32 = jnp.float32
BF16 = jnp.bfloat16
I32 = jnp.int32
SMEM = pl.BlockSpec(memory_space=pltpu.SMEM)
VMEM = pl.BlockSpec(memory_space=pltpu.VMEM)
ANY = pl.BlockSpec(memory_space=pl.ANY)


def prepare_kernel(rows_ref, charges_ref, p2m_ref, m2m_ref, mult_ref, parent_ref, out_ref, wide, block):
    mult = jnp.dot(charges_ref[...], p2m_ref[...], preferred_element_type=F32).astype(BF16)
    mult_ref[...] = mult
    wide[...] = mult.astype(F32)
    parents = parent_ref.shape[0]
    total = jnp.zeros(parent_ref.shape, F32)
    for octant in range(8):
        child = wide[pl.ds(octant, parents, stride=8), :].astype(BF16)
        total = total + jnp.dot(child, m2m_ref[octant], preferred_element_type=F32)
    parent_ref[...] = total.astype(BF16)
    step = block.shape[0]

    def some(g, carry):
        rows = rows_ref.at[pl.ds(g * step, step)]
        for u in range(step):
            block[pl.ds(u, 1), :] = wide[pl.ds(rows[u], 1), :]
        out_ref[pl.ds(pl.multiple_of(g * step, step), step), :] = block[...].astype(BF16)
        return carry

    lax.fori_loop(0, out_ref.shape[0] // step, some, 0)


def prepare(rows, charges, p2m, m2m):
    leaf_dev, coeffs = charges.shape[0], p2m.shape[1]
    return pl.pallas_call(
        prepare_kernel,
        out_shape=(
            jax.ShapeDtypeStruct((leaf_dev, coeffs), BF16),
            jax.ShapeDtypeStruct((leaf_dev // 8, coeffs), BF16),
            jax.ShapeDtypeStruct((rows.shape[0], coeffs), BF16),
        ),
        in_specs=[SMEM, VMEM, VMEM, VMEM],
        out_specs=(VMEM, VMEM, VMEM),
        scratch_shapes=[pltpu.VMEM((leaf_dev, coeffs), F32), pltpu.VMEM((128, coeffs), F32)],
        compiler_params=pltpu.CompilerParams(vmem_limit_bytes=32 << 20),
        name="prepare",
    )(rows, charges, p2m, m2m)


Z_SCALE = 2.0**-10
EDGE = 8
MESH = pl.DeviceIdType.MESH


def exchange_kernel(
    n_sec, n_sub, out_ref, parent_ref, pos_ref, charge_ref, list_ref, arrived_ref, parents_ref, near_ref,
    edge, halo, xy, zq, send_sems, recv_sems, own_sems,
):
    devices = n_sec * n_sub
    me = lax.axis_index("sec") * n_sub + lax.axis_index("sub")
    cap = out_ref.shape[0] // devices
    share = parent_ref.shape[0]
    leaf_dev, panels = near_ref.shape

    def place_of(device):
        return (device // n_sub, device % n_sub)

    def other(distance):
        return (me + distance) % devices

    barrier = pltpu.get_barrier_semaphore()

    def greet(d, carry):
        pl.semaphore_signal(barrier, inc=1, device_id=place_of(other(d)), device_id_type=MESH)
        return carry

    lax.fori_loop(1, devices, greet, 0)
    for side, rows in ((0, pl.ds(leaf_dev - EDGE, EDGE)), (1, pl.ds(0, EDGE))):
        for axis in range(3):
            edge[side, axis] = pos_ref[axis, rows, :]
    charges = charge_ref[...].astype(F32)
    edge[0, 3] = charges[leaf_dev - EDGE :]
    edge[1, 3] = charges[:EDGE]
    pl.semaphore_wait(barrier, devices - 1)

    def to_side(side):
        return pltpu.make_async_remote_copy(
            src_ref=edge.at[side], dst_ref=halo.at[side], send_sem=send_sems.at[side], recv_sem=recv_sems.at[side],
            device_id=place_of(other(1 if side == 0 else devices - 1)), device_id_type=MESH,
        )

    def send(source, target, which, device):
        return pltpu.make_async_remote_copy(
            src_ref=source, dst_ref=target, send_sem=send_sems.at[which], recv_sem=recv_sems.at[which],
            device_id=place_of(device), device_id_type=MESH,
        )

    to_side(0).start()
    to_side(1).start()
    mine = pl.ds(pl.multiple_of(me * cap, cap), cap)
    mine_up = pl.ds(pl.multiple_of(me * share, share), share)

    def give(d, carry):
        device = other(d)
        send(out_ref.at[pl.ds(pl.multiple_of(device * cap, cap), cap), :], arrived_ref.at[mine, :], 2, device).start()
        send(parent_ref, parents_ref.at[mine_up, :], 3, device).start()
        return carry

    lax.fori_loop(1, devices, give, 0)
    own = pltpu.make_async_copy(out_ref.at[mine, :], arrived_ref.at[mine, :], own_sems.at[0])
    own_up = pltpu.make_async_copy(parent_ref, parents_ref.at[mine_up, :], own_sems.at[1])
    own.start()
    own_up.start()

    def store(x, y, z, q, first, count):
        whole_x = jnp.round(x * 65535.0).astype(I32) - 32768
        whole_y = jnp.round(y * 65535.0).astype(I32)
        xy[pl.ds(first, count), :] = whole_x * 65536 + whole_y
        zq[pl.ds(first, count), :] = q * (1.0 + (z - 0.5) * Z_SCALE)

    store(pos_ref[0], pos_ref[1], pos_ref[2], charges, EDGE, leaf_dev)
    for side, end, first in ((0, 0, 0), (1, devices - 1, EDGE + leaf_dev)):
        to_side(side).wait()
        strength = halo[side, 3] * jnp.where(me == end, 0.0, 1.0)
        store(halo[side, 0], halo[side, 1], halo[side, 2], strength, first, EDGE)
    lane = lax.broadcasted_iota(I32, (8, panels), 1)
    rim = RIM // panels

    def group(g, carry):
        base = pl.multiple_of(g * 8, 8)
        x = pos_ref[0, pl.ds(base, 8), :]
        y = pos_ref[1, pl.ds(base, 8), :]
        z = pos_ref[2, pl.ds(base, 8), :]
        total = jnp.zeros((8, panels), F32)
        for n in range(list_ref.shape[0]):
            target = list_ref[n, pl.ds(base, 8), :] + lane
            which = target >> 7
            place = target & (panels - 1)
            word = jnp.zeros((8, panels), I32)
            weight = jnp.zeros((8, panels), F32)
            for q in range(2 * rim + 1):
                at = which == q
                rows = pl.ds(base + (EDGE - rim + q), 8)
                word = jnp.where(at, jnp.take_along_axis(xy[rows, :], place, axis=1), word)
                weight = jnp.where(at, jnp.take_along_axis(zq[rows, :], place, axis=1), weight)
            strength = weight.astype(BF16).astype(F32)
            safe = jnp.where(strength == 0.0, 1.0, strength)
            far_z = (weight - strength) / safe * (1.0 / Z_SCALE) + 0.5
            far_x = ((word >> 16) + 32768).astype(F32) * (1.0 / 65535.0)
            far_y = (word & 65535).astype(F32) * (1.0 / 65535.0)
            dx, dy, dz = x - far_x, y - far_y, z - far_z
            total = total + strength * lax.rsqrt(dx * dx + dy * dy + dz * dz + SOFT)
        near_ref[pl.ds(base, 8), :] = total * (1.0 / list_ref.shape[0])
        return carry

    lax.fori_loop(0, leaf_dev // 8, group, 0)
    own.wait()
    own_up.wait()
    rest = pl.ds(0, (devices - 1) * cap)
    rest_up = pl.ds(0, (devices - 1) * share)
    all_leaves = send(out_ref.at[rest, :], arrived_ref.at[rest, :], 2, other(1))
    all_leaves.wait_recv()
    all_leaves.wait_send()
    all_parents = send(parents_ref.at[rest_up, :], parents_ref.at[rest_up, :], 3, other(1))
    all_parents.wait_recv()
    all_parents.wait_send()


def exchange(n_sec, n_sub, outgoing, parent_own, positions, charges, near_list):
    leaf_dev, panels = charges.shape
    coeffs = outgoing.shape[1]
    devices = n_sec * n_sub
    full = leaf_dev + 2 * EDGE
    return pl.pallas_call(
        functools.partial(exchange_kernel, n_sec, n_sub),
        out_shape=(
            jax.ShapeDtypeStruct(outgoing.shape, BF16),
            jax.ShapeDtypeStruct((devices * parent_own.shape[0], coeffs), BF16),
            jax.ShapeDtypeStruct((leaf_dev, panels), F32),
        ),
        in_specs=[VMEM] * 5,
        out_specs=(VMEM, VMEM, VMEM),
        scratch_shapes=[
            pltpu.VMEM((2, 4, EDGE, panels), F32),
            pltpu.VMEM((2, 4, EDGE, panels), F32),
            pltpu.VMEM((full, panels), I32),
            pltpu.VMEM((full, panels), F32),
            pltpu.SemaphoreType.DMA((4,)),
            pltpu.SemaphoreType.DMA((4,)),
            pltpu.SemaphoreType.DMA((2,)),
        ],
        compiler_params=pltpu.CompilerParams(vmem_limit_bytes=32 << 20, collective_id=0, has_side_effects=True),
        name="exchange",
    )(outgoing, parent_own, positions, charges, near_list)


GROUP = 16
QUAD = 4


def far_kernel(
    leaf_list_ref, parent_list_ref, leaf_types_ref, parent_types_ref, arrived_ref, own_ref, parents_ref,
    m2l_hbm, l2l_ref, l2p_ref, near_ref, out_ref,
    table, lists, types, rows, tall_a, tall_b, grouped, m2l, total, index_a, index_b, sems,
):
    leaf_dev = leaf_list_ref.shape[0]
    boxes, entries = lists.shape
    wide = rows.shape[0] // GROUP
    kinds, coeffs = m2l.shape[0], m2l.shape[2]
    steps = boxes // GROUP
    weights = pltpu.make_async_copy(m2l_hbm, m2l, sems.at[2])
    weights.start()
    leaf_rows = arrived_ref.shape[0] + own_ref.shape[0]
    lists[pl.ds(0, leaf_dev), :] = leaf_list_ref[...]
    lists[pl.ds(leaf_dev, boxes - leaf_dev), :] = parent_list_ref[...] + leaf_rows

    def fetch(step, buffer, which):
        at = pl.multiple_of(step * GROUP, GROUP)
        return pltpu.make_async_copy(lists.at[pl.ds(at, GROUP), :], buffer, sems.at[which])

    fetch(0, index_a, 0).start()
    fetch(1, index_b, 1).start()
    types[...] = jnp.full_like(types, -1)
    types[pl.ds(0, leaf_dev), pl.ds(0, entries)] = leaf_types_ref[...]
    types[pl.ds(leaf_dev, boxes - leaf_dev), pl.ds(0, entries)] = parent_types_ref[...]
    rows[...] = jnp.zeros_like(rows)
    tall_b[...] = jnp.zeros_like(tall_b)
    first = 0
    for source in (arrived_ref, own_ref, parents_ref):
        count = source.shape[0]
        table[pl.ds(first, count), :] = source[...].astype(F32)
        first += count
    kinds_up = tall_a.shape[1] // QUAD - 4
    kind_of = lax.broadcasted_iota(I32, (kinds_up, types.shape[1]), 0)
    upper = lax.broadcasted_iota(I32, (8, coeffs), 0) >= QUAD

    def pick(index):
        for box in range(GROUP):
            for k in range(entries):
                rows[pl.ds(box * wide + k, 1), :] = table[pl.ds(index[box, k], 1), :]

    def spread(tall, step):
        for box in range(GROUP):
            kind = types[pl.ds(step * GROUP + box, 1), :]
            onehot = (kind_of == kind).astype(BF16)
            picked = rows[pl.ds(box * wide, wide), :].astype(BF16)
            tall[box // QUAD, pl.ds(8 + box % QUAD, kinds_up, stride=QUAD), :] = jnp.dot(
                onehot, picked, preferred_element_type=F32
            )

    def turn(tall, step):
        at = pl.multiple_of(step * GROUP, GROUP)
        for t in range(kinds):
            pair = [
                jnp.where(upper, tall[2 * h + 1, pl.ds(8 + t * QUAD - QUAD, 8), :], tall[2 * h, pl.ds(8 + t * QUAD, 8), :])
                for h in range(2)
            ]
            grouped[t, pl.ds(at, GROUP), :] = jnp.concatenate(pair, 0).astype(BF16)

    def some(i, carry):
        for half, index, tall, done in ((0, index_a, tall_a, tall_b), (1, index_b, tall_b, tall_a)):
            step = i * 2 + half
            fetch(step, index, half).wait()
            pick(index)
            spread(tall, step)
            turn(done, jnp.maximum(step - 1, 0))
            fetch(jnp.minimum(step + 2, steps - 2 + half), index, half).start()
        return carry

    lax.fori_loop(0, steps // 2, some, 0)
    for half, index in ((0, index_a), (1, index_b)):
        fetch(steps - 2 + half, index, half).wait()
    turn(tall_b, steps - 1)
    weights.wait()
    total[...] = jnp.zeros_like(total)
    chunk = 12

    def multiply(first, count):
        left = jnp.concatenate([grouped[first + t] for t in range(count)], axis=1)
        right = m2l[pl.ds(first, count)].reshape(count * coeffs, coeffs)
        total[...] += jnp.dot(left, right, preferred_element_type=F32)

    def several(i, carry):
        multiply(i * chunk, chunk)
        return carry

    lax.fori_loop(0, kinds // chunk, several, 0)
    if kinds % chunk:
        multiply(kinds // chunk * chunk, kinds % chunk)
    parents = boxes - leaf_dev
    parent_local = total[pl.ds(leaf_dev, parents), :].astype(BF16)
    for octant in range(8):
        down = jnp.dot(parent_local, l2l_ref[octant], preferred_element_type=F32)
        total[pl.ds(octant, parents, stride=8), :] += down
    leaf_total = total[pl.ds(0, leaf_dev), :].astype(BF16)
    out_ref[...] = jnp.dot(leaf_total, l2p_ref[...], preferred_element_type=F32) + near_ref[...]


def far_field(leaf_list, parent_list, leaf_types, parent_types, arrived, own, parents, m2l, l2l, l2p, near):
    boxes, entries = leaf_list.shape[0] + parent_list.shape[0], leaf_list.shape[1]
    kinds, coeffs = m2l.shape[0], m2l.shape[2]
    tables = arrived.shape[0] + own.shape[0] + parents.shape[0]
    wide = -(-entries // 16) * 16
    kinds_up = -(-kinds // 16) * 16
    return pl.pallas_call(
        far_kernel,
        out_shape=jax.ShapeDtypeStruct(near.shape, F32),
        in_specs=[VMEM] * 7 + [ANY] + [VMEM] * 3,
        out_specs=VMEM,
        scratch_shapes=[
            pltpu.VMEM((tables, coeffs), F32),
            pltpu.VMEM((boxes, entries), I32),
            pltpu.VMEM((boxes, wide), I32),
            pltpu.VMEM((GROUP * wide, coeffs), F32),
            pltpu.VMEM((GROUP // QUAD, kinds_up * QUAD + 4 * QUAD, coeffs), F32),
            pltpu.VMEM((GROUP // QUAD, kinds_up * QUAD + 4 * QUAD, coeffs), F32),
            pltpu.VMEM((kinds, boxes, coeffs), BF16),
            pltpu.VMEM(m2l.shape, BF16),
            pltpu.VMEM((boxes, coeffs), F32),
            pltpu.SMEM((GROUP, entries), I32),
            pltpu.SMEM((GROUP, entries), I32),
            pltpu.SemaphoreType.DMA((3,)),
        ],
        compiler_params=pltpu.CompilerParams(vmem_limit_bytes=58 << 20),
        name="far",
    )(leaf_list, parent_list, leaf_types, parent_types, arrived, own, parents, m2l, l2l, l2p, near)


def local(
    charges, positions, p2m, m2m, m2l, l2l, l2p,
    send_rows, send_counts, leaf_list, leaf_types, parent_list, parent_types, near_list,
):
    n_sec, n_sub = lax.axis_size("sec"), lax.axis_size("sub")
    own, parent_own, outgoing = prepare(send_rows.reshape(n_sec * n_sub * send_rows.shape[2]), charges, p2m, m2m)
    arrived, parents, near = exchange(n_sec, n_sub, outgoing, parent_own, positions, charges, near_list)
    return far_field(leaf_list, parent_list, leaf_types, parent_types, arrived, own, parents, m2l, l2l, l2p, near)


def solution(mesh):
    along = P(BOTH, None)
    in_specs = (
        along, P(None, BOTH, None), P(), P(), P(), P(), P(),
        P(BOTH, None, None), along, along, along, along, along, P(None, BOTH, None),
    )
    return jax.shard_map(local, mesh=mesh, in_specs=in_specs, out_specs=along, check_vma=False)
```

time: 161 us -> 140 us (0.87)
  the two profiles are of different devices: /device:TPU:1 before, /device:TPU:29 now
where the time goes in v2:
time: 140 us; the launch traced here: 139 us
  Pallas kernels  126 us (90%)
  local copies, waits for them, and re-layouts  13.6 us (10%)
    pallas_call x1, Pallas kernels, far_field(): pl.pallas_call(far_kernel, out_shape=jax.ShapeDtypeStruct(near.shape, F32...  66 us
    pallas_call x1, Pallas kernels, exchange(): pl.pallas_call(functools.partial(exchange_kernel, n_sec, n_sub), out_shap...  54.5 us
    unnamed x23, local copies, waits for them, and re-layouts  13.5 us
    pallas_call x1, Pallas kernels, prepare(): pl.pallas_call(prepare_kernel, out_shape=(jax.ShapeDtypeStruct((leaf_dev,...  4.99 us

profile of v2, /device:TPU:29, one launch (start us, length us, event | category | flops | bytes accessed | tf_op | source)
XLA Modules:
  0.0 139.2 jit_solution(16555743847193972555)
XLA Ops:
  0.0 0.8 copy.16
  0.8 0.1 reshape.3.rows_ref
  0.9 0.0 copy-start.4
  0.9 0.8 copy-done.4
  1.7 0.0 copy-start.6
  1.7 0.9 copy-done.6
  2.7 0.0 copy-start.9
  2.7 0.8 copy-done.9
  3.4 5.0 %prepare.1 = (bf16[256,128]{1,0:T(8,128)(2,1)S(1)}, bf16[32,128]{1,0:T(8,128)(2,1)S(1)}, bf16[4096,128]{1,0:T(8,128)(2,1)S(1)}) custom-call(s32[4096]{0:T(1024)S(1)} %reshape.3.rows_ref, bf16[256,128]{1,0:T(8,128)(2,1)S(1)} %copy-done.4, bf16[128,128]{1,0:T(8,128)(2,1)S(1)} %copy-done.9, bf16[8,128,128]{2,1,0:T(8,128)(2,1)S(1)} %copy-done.6), custom_call_target="tpu_custom_call" | custom-call | tf_op jit(solution)/shard_map/prepare/pallas_call | solution.py:45
  8.4 0.0 copy-start.8
  8.4 0.6 copy-done.8
  9.1 0.0 copy-start
  9.1 1.6 %copy-done = s32[16,256,128]{2,1,0:T(8,128)S(1)} copy-done((s32[16,256,128]{2,1,0:T(8,128)S(1)}, s32[16,256,128]{2,1,0:T(8,128)}, u32[]{:S(2)}) %copy-start) | copy-done | bytes 2097176
  10.7 0.0 copy-start.3
  10.7 1.0 copy-done.3
  11.6 0.0 copy-start.5
  11.6 0.8 copy-done.5
  12.5 54.5 %exchange.1 = (bf16[4096,128]{1,0:T(8,128)(2,1)S(1)}, bf16[4096,128]{1,0:T(8,128)(2,1)S(1)}, f32[256,128]{1,0:T(8,128)S(1)}) custom-call(bf16[4096,128]{1,0:T(8,128)(2,1)S(1)} %get-tuple-element.11.out_ref, bf16[32,128]{1,0:T(8,128)(2,1)S(1)} %get-tuple-element.12.parent_ref, f32[3,256,128]{2,1,0:T(8,128)S(1)} %copy-done.3, bf16[256,128]{1,0:T(8,128)(2,1)S(1)} %copy-done.5, ...), custom_call_target="tpu_custom_call" | custom-call | tf_op jit(solution)/shard_map/exchange/pallas_call | solution.py:184
  67.0 0.0 copy-start.1
  67.0 1.0 copy-done.1
  68.0 0.0 copy-start.2
  68.0 1.0 copy-done.2
  69.0 0.0 copy-start.7
  69.0 0.7 copy-done.7
  69.6 1.8 %copy.17.leaf_list_ref = s32[256,189]{1,0:T(8,128)} copy(s32[256,189]{0,1:T(8,128)} %param.22) | data formatting | bytes 387072 | tf_op args[9]
  71.4 1.8 %copy.18.leaf_types_ref = s32[256,189]{1,0:T(8,128)} copy(s32[256,189]{0,1:T(8,128)} %param.23) | data formatting | bytes 387072 | tf_op args[10]
  73.1 66.0 %far.1 = f32[256,128]{1,0:T(8,128)} custom-call(s32[256,189]{1,0:T(8,128)} %copy.17.leaf_list_ref, s32[32,189]{1,0:T(8,128)} %parent_list_ref.1, s32[256,189]{1,0:T(8,128)} %copy.18.leaf_types_ref, s32[32,189]{1,0:T(8,128)} %parent_types_ref.1, bf16[4096,128]{1,0:T(8,128)(2,1)} %copy-done.1, bf16[256,128]{1,0:T(8,128)(2,1)} %copy-done.8, ...), custom_call_target="tpu_custom_call" | custom-call | tf_op jit(solution)/shard_map/far/pallas_call | solution.py:315
Async XLA Ops:
  0.9 0.8 copy-start.4
  1.7 0.9 copy-start.6
  2.7 0.8 copy-start.9
  8.4 0.6 copy-start.8
  9.1 1.6 %copy-start = (s32[16,256,128]{2,1,0:T(8,128)S(1)}, s32[16,256,128]{2,1,0:T(8,128)}, u32[]{:S(2)}) copy-start(s32[16,256,128]{2,1,0:T(8,128)} %list_ref.1) | copy-start | bytes 6291460
  10.7 1.0 copy-start.3
  11.6 0.8 copy-start.5
  67.0 1.0 copy-start.1
  68.0 1.0 copy-start.2
  69.0 0.7 copy-start.7

commit v3 on v2

v3 whole, which is shorter than its diff:
```python
import functools

import jax
import jax.numpy as jnp
from jax import lax
from jax.experimental import pallas as pl
from jax.experimental.pallas import tpu as pltpu
from jax.sharding import PartitionSpec as P

RIM = 512
SOFT = 0.0025
BOTH = ("sec", "sub")
F32 = jnp.float32
BF16 = jnp.bfloat16
I32 = jnp.int32
SMEM = pl.BlockSpec(memory_space=pltpu.SMEM)
VMEM = pl.BlockSpec(memory_space=pltpu.VMEM)
ANY = pl.BlockSpec(memory_space=pl.ANY)


Z_SCALE = 2.0**-10
EDGE = 8
STRIDE = 37
MESH = pl.DeviceIdType.MESH


def exchange_kernel(
    n_sec, n_sub, rows_ref, charge_hbm, p2m_hbm, m2m_hbm, pos_hbm, list_hbm, own_ref, arrived_ref, parents_ref, near_ref,
    charge_ref, p2m_ref, m2m_ref, pos_ref, list_ref, wide, block, out_ref, parent_ref,
    edge, halo, xy, zq, in_sems, send_sems, recv_sems, own_sems,
):
    devices = n_sec * n_sub
    me = lax.axis_index("sec") * n_sub + lax.axis_index("sub")
    chip, core = me // 2, me % 2
    chips = devices // 2
    cap = out_ref.shape[0] // devices
    leaf_dev, panels = near_ref.shape

    def place_of(device):
        return (device // n_sub, device % n_sub)

    def other(distance):
        return (me + distance) % devices

    loads = [
        pltpu.make_async_copy(source, target, in_sems.at[i])
        for i, (source, target) in enumerate(
            ((charge_hbm, charge_ref), (p2m_hbm, p2m_ref), (m2m_hbm, m2m_ref), (pos_hbm, pos_ref), (list_hbm, list_ref))
        )
    ]
    for load in loads:
        load.start()
    barrier = pltpu.get_barrier_semaphore()

    def greet(d, carry):
        pl.semaphore_signal(barrier, inc=1, device_id=place_of(other((d * STRIDE) % devices)), device_id_type=MESH)
        return carry

    lax.fori_loop(1, devices, greet, 0)
    for load in loads[:3]:
        load.wait()
    mult = jnp.dot(charge_ref[...], p2m_ref[...], preferred_element_type=F32).astype(BF16)
    own_ref[...] = mult
    wide[...] = mult.astype(F32)
    share = parent_ref.shape[0]
    total = jnp.zeros(parent_ref.shape, F32)
    for octant in range(8):
        child = wide[pl.ds(octant, share, stride=8), :].astype(BF16)
        total = total + jnp.dot(child, m2m_ref[octant], preferred_element_type=F32)
    parent_ref[...] = total.astype(BF16)
    step = block.shape[0]

    def some(g, carry):
        rows = rows_ref.at[pl.ds(g * step, step)]
        for u in range(step):
            block[pl.ds(u, 1), :] = wide[pl.ds(rows[u], 1), :]
        out_ref[pl.ds(pl.multiple_of(g * step, step), step), :] = block[...].astype(BF16)
        return carry

    lax.fori_loop(0, out_ref.shape[0] // step, some, 0)
    loads[3].wait()
    for side, rows in ((0, pl.ds(leaf_dev - EDGE, EDGE)), (1, pl.ds(0, EDGE))):
        for axis in range(3):
            edge[side, axis] = pos_ref[axis, rows, :]
    charges = charge_ref[...].astype(F32)
    edge[0, 3] = charges[leaf_dev - EDGE :]
    edge[1, 3] = charges[:EDGE]
    pl.semaphore_wait(barrier, devices - 1)

    def send(source, target, which, device):
        return pltpu.make_async_remote_copy(
            src_ref=source, dst_ref=target, send_sem=send_sems.at[which], recv_sem=recv_sems.at[which],
            device_id=place_of(device), device_id_type=MESH,
        )

    def to_side(side):
        return send(edge.at[side], halo.at[side], side, other(1 if side == 0 else devices - 1))

    to_side(0).start()
    to_side(1).start()
    mine = pl.ds(pl.multiple_of(me * cap, cap), cap)

    def give_up(d, carry):
        send(parent_ref, parents_ref.at[chip, core], 3, other((2 * d * STRIDE) % devices)).start()
        return carry

    def give(d, carry):
        device = other((d * STRIDE) % devices)
        send(out_ref.at[pl.ds(pl.multiple_of(device * cap, cap), cap), :], arrived_ref.at[mine, :], 2, device).start()
        return carry

    lax.fori_loop(1, chips, give_up, 0)
    lax.fori_loop(1, devices, give, 0)
    own = pltpu.make_async_copy(out_ref.at[mine, :], arrived_ref.at[mine, :], own_sems.at[0])
    own_up = pltpu.make_async_copy(parent_ref, parents_ref.at[chip, core], own_sems.at[1])
    own.start()
    own_up.start()
    loads[4].wait()

    def store(x, y, z, q, first, count):
        whole_x = jnp.round(x * 65535.0).astype(I32) - 32768
        whole_y = jnp.round(y * 65535.0).astype(I32)
        xy[pl.ds(first, count), :] = whole_x * 65536 + whole_y
        zq[pl.ds(first, count), :] = q * (1.0 + (z - 0.5) * Z_SCALE)

    store(pos_ref[0], pos_ref[1], pos_ref[2], charges, EDGE, leaf_dev)
    for side, end, first in ((0, 0, 0), (1, devices - 1, EDGE + leaf_dev)):
        to_side(side).wait()
        strength = halo[side, 3] * jnp.where(me == end, 0.0, 1.0)
        store(halo[side, 0], halo[side, 1], halo[side, 2], strength, first, EDGE)
    lane = lax.broadcasted_iota(I32, (8, panels), 1)
    rim = RIM // panels

    def group(g, carry):
        base = pl.multiple_of(g * 8, 8)
        x = pos_ref[0, pl.ds(base, 8), :]
        y = pos_ref[1, pl.ds(base, 8), :]
        z = pos_ref[2, pl.ds(base, 8), :]
        total = jnp.zeros((8, panels), F32)
        for n in range(list_ref.shape[0]):
            target = list_ref[n, pl.ds(base, 8), :] + lane
            which = target >> 7
            place = target & (panels - 1)
            word = jnp.zeros((8, panels), I32)
            weight = jnp.zeros((8, panels), F32)
            for q in range(2 * rim + 1):
                at = which == q
                rows = pl.ds(base + (EDGE - rim + q), 8)
                word = jnp.where(at, jnp.take_along_axis(xy[rows, :], place, axis=1), word)
                weight = jnp.where(at, jnp.take_along_axis(zq[rows, :], place, axis=1), weight)
            strength = weight.astype(BF16).astype(F32)
            safe = jnp.where(strength == 0.0, 1.0, strength)
            far_z = (weight - strength) / safe * (1.0 / Z_SCALE) + 0.5
            far_x = ((word >> 16) + 32768).astype(F32) * (1.0 / 65535.0)
            far_y = (word & 65535).astype(F32) * (1.0 / 65535.0)
            dx, dy, dz = x - far_x, y - far_y, z - far_z
            total = total + strength * lax.rsqrt(dx * dx + dy * dy + dz * dz + SOFT)
        near_ref[pl.ds(base, 8), :] = total * (1.0 / list_ref.shape[0])
        return carry

    lax.fori_loop(0, leaf_dev // 8, group, 0)
    own_up.wait()
    from_peers = send(parents_ref.at[pl.ds(0, chips - 1), 0], parents_ref.at[pl.ds(0, chips - 1), 0], 3, other(1))
    from_peers.wait_recv()
    sibling = me + 1 - 2 * core
    pass_on = send(parents_ref.at[:, core], parents_ref.at[:, core], 4, sibling)
    pass_on.start()
    from_peers.wait_send()
    own.wait()
    rest = pl.ds(0, (devices - 1) * cap)
    all_leaves = send(out_ref.at[rest, :], arrived_ref.at[rest, :], 2, other(1))
    all_leaves.wait_recv()
    all_leaves.wait_send()
    pass_on.wait()


def exchange(n_sec, n_sub, rows, charges, p2m, m2m, positions, near_list):
    leaf_dev, panels = charges.shape
    coeffs = p2m.shape[1]
    devices = n_sec * n_sub
    full = leaf_dev + 2 * EDGE
    share = leaf_dev // 8
    return pl.pallas_call(
        functools.partial(exchange_kernel, n_sec, n_sub),
        out_shape=(
            jax.ShapeDtypeStruct((leaf_dev, coeffs), BF16),
            jax.ShapeDtypeStruct((rows.shape[0], coeffs), BF16),
            jax.ShapeDtypeStruct((devices // 2, 2, share, coeffs), BF16),
            jax.ShapeDtypeStruct((leaf_dev, panels), F32),
        ),
        in_specs=[SMEM] + [ANY] * 5,
        out_specs=(VMEM, ANY, ANY, VMEM),
        scratch_shapes=[
            pltpu.VMEM(charges.shape, BF16),
            pltpu.VMEM(p2m.shape, BF16),
            pltpu.VMEM(m2m.shape, BF16),
            pltpu.VMEM(positions.shape, F32),
            pltpu.VMEM(near_list.shape, I32),
            pltpu.VMEM((leaf_dev, coeffs), F32),
            pltpu.VMEM((128, coeffs), F32),
            pltpu.VMEM((rows.shape[0], coeffs), BF16),
            pltpu.VMEM((share, coeffs), BF16),
            pltpu.VMEM((2, 4, EDGE, panels), F32),
            pltpu.VMEM((2, 4, EDGE, panels), F32),
            pltpu.VMEM((full, panels), I32),
            pltpu.VMEM((full, panels), F32),
            pltpu.SemaphoreType.DMA((5,)),
            pltpu.SemaphoreType.DMA((5,)),
            pltpu.SemaphoreType.DMA((5,)),
            pltpu.SemaphoreType.DMA((2,)),
        ],
        compiler_params=pltpu.CompilerParams(vmem_limit_bytes=58 << 20, collective_id=0, has_side_effects=True),
        name="exchange",
    )(rows, charges, p2m, m2m, positions, near_list)


GROUP = 16
QUAD = 4


def far_kernel(
    leaf_list_hbm, parent_list_ref, leaf_types_hbm, parent_types_ref, arrived_hbm, own_hbm, parents_hbm,
    m2l_hbm, l2l_hbm, l2p_hbm, near_hbm, out_ref,
    table, lists, types, tall_a, tall_b, grouped, m2l, total, flat_list, flat_types, square, narrow, l2l_ref, l2p_ref, near_ref,
    index_a, index_b, sems, in_sems,
):
    leaf_dev = out_ref.shape[0]
    boxes, entries = lists.shape
    wide = types.shape[1]
    kinds, coeffs = m2l.shape[0], m2l.shape[2]
    steps = boxes // GROUP
    loads = []
    first = 0
    for source in (arrived_hbm, own_hbm, parents_hbm):
        loads.append((source, narrow.at[pl.ds(first, source.shape[0]), :]))
        first += source.shape[0]
    loads += [(leaf_list_hbm, flat_list), (leaf_types_hbm, flat_types)]
    loads += [(l2l_hbm, l2l_ref), (l2p_hbm, l2p_ref), (near_hbm, near_ref)]
    loads = [pltpu.make_async_copy(source, target, in_sems.at[i]) for i, (source, target) in enumerate(loads)]
    for i in (3, 4, 0, 1, 2):
        loads[i].start()
    weights = pltpu.make_async_copy(m2l_hbm, m2l, sems.at[2])
    weights.start()
    for load in loads[5:]:
        load.start()
    leaf_rows = arrived_hbm.shape[0] + own_hbm.shape[0]
    tall_b[...] = jnp.zeros_like(tall_b)
    lift = 8 - lax.broadcasted_iota(I32, (1, entries), 1) % 8
    loads[3].wait()
    square[pl.ds(0, entries), :] = flat_list[...]
    lists[pl.ds(0, leaf_dev), :] = square[...].T[:, :entries] + lift
    lists[pl.ds(leaf_dev, boxes - leaf_dev), :] = parent_list_ref[...] + (lift + leaf_rows)

    def fetch(step, buffer, which):
        at = pl.multiple_of(step * GROUP, GROUP)
        return pltpu.make_async_copy(lists.at[pl.ds(at, GROUP), :], buffer, sems.at[which])

    fetch(0, index_a, 0).start()
    fetch(1, index_b, 1).start()
    types[...] = jnp.full_like(types, -1)
    loads[4].wait()
    square[pl.ds(0, entries), :] = flat_types[...]
    types[pl.ds(0, leaf_dev), pl.ds(0, entries)] = square[...].T[:, :entries]
    types[pl.ds(leaf_dev, boxes - leaf_dev), pl.ds(0, entries)] = parent_types_ref[...]
    for load in loads[:3]:
        load.wait()
    table[pl.ds(0, 8), :] = jnp.zeros((8, coeffs), F32)
    table[pl.ds(table.shape[0] - 8, 8), :] = jnp.zeros((8, coeffs), F32)
    table[pl.ds(8, narrow.shape[0]), :] = narrow[...].astype(F32)
    kinds_up = tall_a.shape[1] // QUAD - 4
    kind_of = lax.broadcasted_iota(I32, (kinds_up, types.shape[1]), 0)
    sub = lax.broadcasted_iota(I32, (8, coeffs), 0)
    upper = lax.broadcasted_iota(I32, (8, coeffs), 0) >= QUAD

    def spread(index, tall, step):
        for box in range(GROUP):
            kind = types[pl.ds(step * GROUP + box, 1), :]
            onehot = (kind_of == kind).astype(BF16)
            tiles = []
            for v in range(wide // 8):
                tile = None
                for r in range(8):
                    if v * 8 + r < entries:
                        row = table[pl.ds(index[box, v * 8 + r], 8), :]
                        tile = row if tile is None else jnp.where(sub == r, row, tile)
                tiles.append(tile)
            picked = jnp.concatenate(tiles, 0).astype(BF16)
            tall[box // QUAD, pl.ds(8 + box % QUAD, kinds_up, stride=QUAD), :] = jnp.dot(
                onehot, picked, preferred_element_type=F32
            )

    def turn(tall, step):
        at = pl.multiple_of(step * GROUP, GROUP)
        for t in range(kinds):
            pair = [
                jnp.where(upper, tall[2 * h + 1, pl.ds(8 + t * QUAD - QUAD, 8), :], tall[2 * h, pl.ds(8 + t * QUAD, 8), :])
                for h in range(2)
            ]
            grouped[t, pl.ds(at, GROUP), :] = jnp.concatenate(pair, 0).astype(BF16)

    def some(i, carry):
        for half, index, tall, done in ((0, index_a, tall_a, tall_b), (1, index_b, tall_b, tall_a)):
            step = i * 2 + half
            fetch(step, index, half).wait()
            spread(index, tall, step)
            turn(done, jnp.maximum(step - 1, 0))
            fetch(jnp.minimum(step + 2, steps - 2 + half), index, half).start()
        return carry

    lax.fori_loop(0, steps // 2, some, 0)
    for half, index in ((0, index_a), (1, index_b)):
        fetch(steps - 2 + half, index, half).wait()
    turn(tall_b, steps - 1)
    weights.wait()
    for load in loads[5:]:
        load.wait()
    total[...] = jnp.zeros_like(total)
    chunk = 12

    def multiply(first, count):
        left = jnp.concatenate([grouped[first + t] for t in range(count)], axis=1)
        right = m2l[pl.ds(first, count)].reshape(count * coeffs, coeffs)
        total[...] += jnp.dot(left, right, preferred_element_type=F32)

    def several(i, carry):
        multiply(i * chunk, chunk)
        return carry

    lax.fori_loop(0, kinds // chunk, several, 0)
    if kinds % chunk:
        multiply(kinds // chunk * chunk, kinds % chunk)
    parents = boxes - leaf_dev
    parent_local = total[pl.ds(leaf_dev, parents), :].astype(BF16)
    for octant in range(8):
        down = jnp.dot(parent_local, l2l_ref[octant], preferred_element_type=F32)
        total[pl.ds(octant, parents, stride=8), :] += down
    leaf_total = total[pl.ds(0, leaf_dev), :].astype(BF16)
    out_ref[...] = jnp.dot(leaf_total, l2p_ref[...], preferred_element_type=F32) + near_ref[...]


def far_field(leaf_list, parent_list, leaf_types, parent_types, arrived, own, parents, m2l, l2l, l2p, near):
    boxes, entries = leaf_list.shape[0] + parent_list.shape[0], leaf_list.shape[1]
    square = -(-entries // 128) * 128
    kinds, coeffs = m2l.shape[0], m2l.shape[2]
    tables = arrived.shape[0] + own.shape[0] + parents.shape[0]
    wide = -(-entries // 16) * 16
    kinds_up = -(-kinds // 16) * 16
    return pl.pallas_call(
        far_kernel,
        out_shape=jax.ShapeDtypeStruct(near.shape, F32),
        in_specs=[ANY, VMEM, ANY, VMEM] + [ANY] * 7,
        out_specs=VMEM,
        scratch_shapes=[
            pltpu.VMEM((tables + 16, coeffs), F32),
            pltpu.VMEM((boxes, entries), I32),
            pltpu.VMEM((boxes, wide), I32),
            pltpu.VMEM((GROUP // QUAD, kinds_up * QUAD + 4 * QUAD, coeffs), F32),
            pltpu.VMEM((GROUP // QUAD, kinds_up * QUAD + 4 * QUAD, coeffs), F32),
            pltpu.VMEM((kinds, boxes, coeffs), BF16),
            pltpu.VMEM(m2l.shape, BF16),
            pltpu.VMEM((boxes, coeffs), F32),
            pltpu.VMEM((entries, leaf_list.shape[0]), I32),
            pltpu.VMEM((entries, leaf_list.shape[0]), I32),
            pltpu.VMEM((square, leaf_list.shape[0]), I32),
            pltpu.VMEM((tables, coeffs), BF16),
            pltpu.VMEM(l2l.shape, BF16),
            pltpu.VMEM(l2p.shape, BF16),
            pltpu.VMEM(near.shape, F32),
            pltpu.SMEM((GROUP, entries), I32),
            pltpu.SMEM((GROUP, entries), I32),
            pltpu.SemaphoreType.DMA((3,)),
            pltpu.SemaphoreType.DMA((8,)),
        ],
        compiler_params=pltpu.CompilerParams(vmem_limit_bytes=58 << 20),
        name="far",
    )(leaf_list.T, parent_list, leaf_types.T, parent_types, arrived, own, parents, m2l, l2l, l2p, near)


def local(
    charges, positions, p2m, m2m, m2l, l2l, l2p,
    send_rows, send_counts, leaf_list, leaf_types, parent_list, parent_types, near_list,
):
    n_sec, n_sub = lax.axis_size("sec"), lax.axis_size("sub")
    rows = send_rows.reshape(n_sec * n_sub * send_rows.shape[2])
    own, arrived, parents, near = exchange(n_sec, n_sub, rows, charges, p2m, m2m, positions, near_list)
    parents = parents.reshape(parents.shape[0] * parents.shape[1] * parents.shape[2], parents.shape[3])
    return far_field(leaf_list, parent_list, leaf_types, parent_types, arrived, own, parents, m2l, l2l, l2p, near)


def solution(mesh):
    along = P(BOTH, None)
    in_specs = (
        along, P(None, BOTH, None), P(), P(), P(), P(), P(),
        P(BOTH, None, None), along, along, along, along, along, P(None, BOTH, None),
    )
    return jax.shard_map(local, mesh=mesh, in_specs=in_specs, out_specs=along, check_vma=False)
```

time: 140 us -> 96.7 us (0.69)
  the two profiles are of different devices: /device:TPU:29 before, /device:TPU:1 now
where the time goes in v3:
time: 96.7 us; the launch traced here: 96.4 us
  Pallas kernels  94.9 us (98%)
  local copies, waits for them, and re-layouts  1.5 us (2%)
    pallas_call x1, Pallas kernels, far_field(): pl.pallas_call(far_kernel, out_shape=jax.ShapeDtypeStruct(near.shape, F32...  57.2 us
    pallas_call x1, Pallas kernels, exchange(): pl.pallas_call(functools.partial(exchange_kernel, n_sec, n_sub), out_shap...  37.7 us

profile of v3, /device:TPU:1, one launch (start us, length us, event | category | flops | bytes accessed | tf_op | source)
XLA Modules:
  0.0 96.4 jit_solution(9784878328834840760)
XLA Ops:
  0.0 0.8 copy.14
  0.8 0.7 reshape.6.rows_ref
  1.5 37.7 %exchange.1 = (bf16[256,128]{1,0:T(8,128)(2,1)}, bf16[4096,128]{1,0:T(8,128)(2,1)}, bf16[64,2,32,128]{3,2,1,0:T(8,128)(2,1)}, f32[256,128]{1,0:T(8,128)}) custom-call(s32[4096]{0:T(1024)} %reshape.6.rows_ref, bf16[256,128]{1,0:T(8,128)(2,1)} %charge_hbm.1, bf16[128,128]{1,0:T(8,128)(2,1)} %p2m_hbm.1, bf16[8,128,128]{2,1,0:T(8,128)(2,1)} %m2m_hbm.1, ...), custom_call_target="tpu_custom_call" | custom-call | tf_op jit(solution)/shard_map/exchange/pallas_call | solution.py:183
  39.2 57.2 %far.1 = f32[256,128]{1,0:T(8,128)} custom-call(s32[189,256]{1,0:T(8,128)} %bitcast.4, s32[32,189]{1,0:T(8,128)} %parent_list_ref.1, s32[189,256]{1,0:T(8,128)} %bitcast.5, s32[32,189]{1,0:T(8,128)} %parent_types_ref.1, bf16[4096,128]{1,0:T(8,128)(2,1)} %get-tuple-element.9.arrived_hbm, bf16[256,128]{1,0:T(8,128)(2,1)} %get-tuple-element.10.own_hbm, ...), custom_call_target="tpu_custom_call" | custom-call | tf_op jit(solution)/shard_map/far/pallas_call | solution.py:348

commit v4 on v3

--- a/solution.py
+++ b/solution.py
@@ -68,16 +68,6 @@
         child = wide[pl.ds(octant, share, stride=8), :].astype(BF16)
         total = total + jnp.dot(child, m2m_ref[octant], preferred_element_type=F32)
     parent_ref[...] = total.astype(BF16)
-    step = block.shape[0]
-
-    def some(g, carry):
-        rows = rows_ref.at[pl.ds(g * step, step)]
-        for u in range(step):
-            block[pl.ds(u, 1), :] = wide[pl.ds(rows[u], 1), :]
-        out_ref[pl.ds(pl.multiple_of(g * step, step), step), :] = block[...].astype(BF16)
-        return carry
-
-    lax.fori_loop(0, out_ref.shape[0] // step, some, 0)
     loads[3].wait()
     for side, rows in ((0, pl.ds(leaf_dev - EDGE, EDGE)), (1, pl.ds(0, EDGE))):
         for axis in range(3):
@@ -110,6 +100,15 @@
         return carry
 
     lax.fori_loop(1, chips, give_up, 0)
+    step = block.shape[0]
+
+    def some(g, carry):
+        for u in range(step):
+            block[pl.ds(u, 1), :] = wide[pl.ds(rows_ref[u % cap, g * (step // cap) + u // cap], 1), :]
+        out_ref[pl.ds(pl.multiple_of(g * step, step), step), :] = block[...].astype(BF16)
+        return carry
+
+    lax.fori_loop(0, out_ref.shape[0] // step, some, 0)
     lax.fori_loop(1, devices, give, 0)
     own = pltpu.make_async_copy(out_ref.at[mine, :], arrived_ref.at[mine, :], own_sems.at[0])
     own_up = pltpu.make_async_copy(parent_ref, parents_ref.at[chip, core], own_sems.at[1])
@@ -184,7 +183,7 @@
         functools.partial(exchange_kernel, n_sec, n_sub),
         out_shape=(
             jax.ShapeDtypeStruct((leaf_dev, coeffs), BF16),
-            jax.ShapeDtypeStruct((rows.shape[0], coeffs), BF16),
+            jax.ShapeDtypeStruct((rows.size, coeffs), BF16),
             jax.ShapeDtypeStruct((devices // 2, 2, share, coeffs), BF16),
             jax.ShapeDtypeStruct((leaf_dev, panels), F32),
         ),
@@ -198,7 +197,7 @@
             pltpu.VMEM(near_list.shape, I32),
             pltpu.VMEM((leaf_dev, coeffs), F32),
             pltpu.VMEM((128, coeffs), F32),
-            pltpu.VMEM((rows.shape[0], coeffs), BF16),
+            pltpu.VMEM((rows.size, coeffs), BF16),
             pltpu.VMEM((share, coeffs), BF16),
             pltpu.VMEM((2, 4, EDGE, panels), F32),
             pltpu.VMEM((2, 4, EDGE, panels), F32),
@@ -215,7 +214,7 @@
 
 
 GROUP = 16
-QUAD = 4
+QUAD = 8
 
 
 def far_kernel(
@@ -267,10 +266,9 @@
     table[pl.ds(0, 8), :] = jnp.zeros((8, coeffs), F32)
     table[pl.ds(table.shape[0] - 8, 8), :] = jnp.zeros((8, coeffs), F32)
     table[pl.ds(8, narrow.shape[0]), :] = narrow[...].astype(F32)
-    kinds_up = tall_a.shape[1] // QUAD - 4
+    kinds_up = tall_a.shape[1] // QUAD
     kind_of = lax.broadcasted_iota(I32, (kinds_up, types.shape[1]), 0)
     sub = lax.broadcasted_iota(I32, (8, coeffs), 0)
-    upper = lax.broadcasted_iota(I32, (8, coeffs), 0) >= QUAD
 
     def spread(index, tall, step):
         for box in range(GROUP):
@@ -285,17 +283,14 @@
                         tile = row if tile is None else jnp.where(sub == r, row, tile)
                 tiles.append(tile)
             picked = jnp.concatenate(tiles, 0).astype(BF16)
-            tall[box // QUAD, pl.ds(8 + box % QUAD, kinds_up, stride=QUAD), :] = jnp.dot(
+            tall[box // QUAD, pl.ds(box % QUAD, kinds_up, stride=QUAD), :] = jnp.dot(
                 onehot, picked, preferred_element_type=F32
             )
 
     def turn(tall, step):
         at = pl.multiple_of(step * GROUP, GROUP)
         for t in range(kinds):
-            pair = [
-                jnp.where(upper, tall[2 * h + 1, pl.ds(8 + t * QUAD - QUAD, 8), :], tall[2 * h, pl.ds(8 + t * QUAD, 8), :])
-                for h in range(2)
-            ]
+            pair = [tall[h, pl.ds(t * QUAD, QUAD), :] for h in range(GROUP // QUAD)]
             grouped[t, pl.ds(at, GROUP), :] = jnp.concatenate(pair, 0).astype(BF16)
 
     def some(i, carry):
@@ -315,7 +310,7 @@
     for load in loads[5:]:
         load.wait()
     total[...] = jnp.zeros_like(total)
-    chunk = 12
+    chunk = 28
 
     def multiply(first, count):
         left = jnp.concatenate([grouped[first + t] for t in range(count)], axis=1)
@@ -354,8 +349,8 @@
             pltpu.VMEM((tables + 16, coeffs), F32),
             pltpu.VMEM((boxes, entries), I32),
             pltpu.VMEM((boxes, wide), I32),
-            pltpu.VMEM((GROUP // QUAD, kinds_up * QUAD + 4 * QUAD, coeffs), F32),
-            pltpu.VMEM((GROUP // QUAD, kinds_up * QUAD + 4 * QUAD, coeffs), F32),
+            pltpu.VMEM((GROUP // QUAD, kinds_up * QUAD, coeffs), F32),
+            pltpu.VMEM((GROUP // QUAD, kinds_up * QUAD, coeffs), F32),
             pltpu.VMEM((kinds, boxes, coeffs), BF16),
             pltpu.VMEM(m2l.shape, BF16),
             pltpu.VMEM((boxes, coeffs), F32),
@@ -381,8 +376,7 @@
     send_rows, send_counts, leaf_list, leaf_types, parent_list, parent_types, near_list,
 ):
     n_sec, n_sub = lax.axis_size("sec"), lax.axis_size("sub")
-    rows = send_rows.reshape(n_sec * n_sub * send_rows.shape[2])
-    own, arrived, parents, near = exchange(n_sec, n_sub, rows, charges, p2m, m2m, positions, near_list)
+    own, arrived, parents, near = exchange(n_sec, n_sub, send_rows[0].T, charges, p2m, m2m, positions, near_list)
     parents = parents.reshape(parents.shape[0] * parents.shape[1] * parents.shape[2], parents.shape[3])
     return far_field(leaf_list, parent_list, leaf_types, parent_types, arrived, own, parents, m2l, l2l, l2p, near)
 

time: 96.7 us -> 94.9 us (0.981)
  local copies, waits for them, and re-layouts: 1.5 us -> 0 us
    pallas_call x1, Pallas kernels: 57.2 us -> 53 us  [far_field(): pl.pallas_call(far_kernel, out_shape=jax.ShapeDtypeStruct(near.shape, F32...]
    pallas_call x1, Pallas kernels: 37.7 us -> 41.6 us  [exchange(): pl.pallas_call(functools.partial(exchange_kernel, n_sec, n_sub), out_shap...]
where the time goes in v4:
time: 94.9 us; the launch traced here: 94.7 us
  Pallas kernels  94.7 us (100%)
    pallas_call x1, Pallas kernels, far_field(): pl.pallas_call(far_kernel, out_shape=jax.ShapeDtypeStruct(near.shape, F32...  53 us
    pallas_call x1, Pallas kernels, exchange(): pl.pallas_call(functools.partial(exchange_kernel, n_sec, n_sub), out_shap...  41.6 us

profile of v4, /device:TPU:1, one launch (start us, length us, event | category | flops | bytes accessed | tf_op | source)
XLA Modules:
  0.0 94.7 jit_solution(1733293131558893595)
XLA Ops:
  0.0 41.6 %exchange.1 = (bf16[256,128]{1,0:T(8,128)(2,1)}, bf16[4096,128]{1,0:T(8,128)(2,1)}, bf16[64,2,32,128]{3,2,1,0:T(8,128)(2,1)}, f32[256,128]{1,0:T(8,128)}) custom-call(s32[32,128]{1,0:T(8,128)} %bitcast.9, bf16[256,128]{1,0:T(8,128)(2,1)} %charge_hbm.1, bf16[128,128]{1,0:T(8,128)(2,1)} %p2m_hbm.1, bf16[8,128,128]{2,1,0:T(8,128)(2,1)} %m2m_hbm.1, ...), custom_call_target="tpu_custom_call" | custom-call | tf_op jit(solution)/shard_map/exchange/pallas_call | solution.py:182
  41.6 53.0 %far.1 = f32[256,128]{1,0:T(8,128)} custom-call(s32[189,256]{1,0:T(8,128)} %bitcast.7, s32[32,189]{1,0:T(8,128)} %parent_list_ref.1, s32[189,256]{1,0:T(8,128)} %bitcast.8, s32[32,189]{1,0:T(8,128)} %parent_types_ref.1, bf16[4096,128]{1,0:T(8,128)(2,1)} %get-tuple-element.9.arrived_hbm, bf16[256,128]{1,0:T(8,128)(2,1)} %get-tuple-element.10.own_hbm, ...), custom_call_target="tpu_custom_call" | custom-call | tf_op jit(solution)/shard_map/far/pallas_call | solution.py:343

commit v5 on v3

--- a/solution.py
+++ b/solution.py
@@ -215,7 +215,7 @@
 
 
 GROUP = 16
-QUAD = 4
+QUAD = 8
 
 
 def far_kernel(
@@ -267,10 +267,9 @@
     table[pl.ds(0, 8), :] = jnp.zeros((8, coeffs), F32)
     table[pl.ds(table.shape[0] - 8, 8), :] = jnp.zeros((8, coeffs), F32)
     table[pl.ds(8, narrow.shape[0]), :] = narrow[...].astype(F32)
-    kinds_up = tall_a.shape[1] // QUAD - 4
+    kinds_up = tall_a.shape[1] // QUAD
     kind_of = lax.broadcasted_iota(I32, (kinds_up, types.shape[1]), 0)
     sub = lax.broadcasted_iota(I32, (8, coeffs), 0)
-    upper = lax.broadcasted_iota(I32, (8, coeffs), 0) >= QUAD
 
     def spread(index, tall, step):
         for box in range(GROUP):
@@ -285,17 +284,14 @@
                         tile = row if tile is None else jnp.where(sub == r, row, tile)
                 tiles.append(tile)
             picked = jnp.concatenate(tiles, 0).astype(BF16)
-            tall[box // QUAD, pl.ds(8 + box % QUAD, kinds_up, stride=QUAD), :] = jnp.dot(
+            tall[box // QUAD, pl.ds(box % QUAD, kinds_up, stride=QUAD), :] = jnp.dot(
                 onehot, picked, preferred_element_type=F32
             )
 
     def turn(tall, step):
         at = pl.multiple_of(step * GROUP, GROUP)
         for t in range(kinds):
-            pair = [
-                jnp.where(upper, tall[2 * h + 1, pl.ds(8 + t * QUAD - QUAD, 8), :], tall[2 * h, pl.ds(8 + t * QUAD, 8), :])
-                for h in range(2)
-            ]
+            pair = [tall[h, pl.ds(t * QUAD, QUAD), :] for h in range(GROUP // QUAD)]
             grouped[t, pl.ds(at, GROUP), :] = jnp.concatenate(pair, 0).astype(BF16)
 
     def some(i, carry):
@@ -315,7 +311,7 @@
     for load in loads[5:]:
         load.wait()
     total[...] = jnp.zeros_like(total)
-    chunk = 12
+    chunk = 28
 
     def multiply(first, count):
         left = jnp.concatenate([grouped[first + t] for t in range(count)], axis=1)
@@ -354,8 +350,8 @@
             pltpu.VMEM((tables + 16, coeffs), F32),
             pltpu.VMEM((boxes, entries), I32),
             pltpu.VMEM((boxes, wide), I32),
-            pltpu.VMEM((GROUP // QUAD, kinds_up * QUAD + 4 * QUAD, coeffs), F32),
-            pltpu.VMEM((GROUP // QUAD, kinds_up * QUAD + 4 * QUAD, coeffs), F32),
+            pltpu.VMEM((GROUP // QUAD, kinds_up * QUAD, coeffs), F32),
+            pltpu.VMEM((GROUP // QUAD, kinds_up * QUAD, coeffs), F32),
             pltpu.VMEM((kinds, boxes, coeffs), BF16),
             pltpu.VMEM(m2l.shape, BF16),
             pltpu.VMEM((boxes, coeffs), F32),

time: 96.7 us -> 92.5 us (0.957)
  Pallas kernels: 94.9 us -> 90.7 us
    pallas_call x1, Pallas kernels: 57.2 us -> 53 us  [far_field(): pl.pallas_call(far_kernel, out_shape=jax.ShapeDtypeStruct(near.shape, F32...]
where the time goes in v5:
time: 92.5 us; the launch traced here: 92.3 us
  Pallas kernels  90.7 us (98%)
  local copies, waits for them, and re-layouts  1.5 us (2%)
    pallas_call x1, Pallas kernels, far_field(): pl.pallas_call(far_kernel, out_shape=jax.ShapeDtypeStruct(near.shape, F32...  53 us
    pallas_call x1, Pallas kernels, exchange(): pl.pallas_call(functools.partial(exchange_kernel, n_sec, n_sub), out_shap...  37.7 us

profile of v5, /device:TPU:1, one launch (start us, length us, event | category | flops | bytes accessed | tf_op | source)
XLA Modules:
  0.0 92.3 jit_solution(9242944790697981750)
XLA Ops:
  0.0 0.8 copy.14
  0.8 0.7 reshape.6.rows_ref
  1.5 37.7 %exchange.1 = (bf16[256,128]{1,0:T(8,128)(2,1)}, bf16[4096,128]{1,0:T(8,128)(2,1)}, bf16[64,2,32,128]{3,2,1,0:T(8,128)(2,1)}, f32[256,128]{1,0:T(8,128)}) custom-call(s32[4096]{0:T(1024)} %reshape.6.rows_ref, bf16[256,128]{1,0:T(8,128)(2,1)} %charge_hbm.1, bf16[128,128]{1,0:T(8,128)(2,1)} %p2m_hbm.1, bf16[8,128,128]{2,1,0:T(8,128)(2,1)} %m2m_hbm.1, ...), custom_call_target="tpu_custom_call" | custom-call | tf_op jit(solution)/shard_map/exchange/pallas_call | solution.py:183
  39.2 53.0 %far.1 = f32[256,128]{1,0:T(8,128)} custom-call(s32[189,256]{1,0:T(8,128)} %bitcast.4, s32[32,189]{1,0:T(8,128)} %parent_list_ref.1, s32[189,256]{1,0:T(8,128)} %bitcast.5, s32[32,189]{1,0:T(8,128)} %parent_types_ref.1, bf16[4096,128]{1,0:T(8,128)(2,1)} %get-tuple-element.9.arrived_hbm, bf16[256,128]{1,0:T(8,128)(2,1)} %get-tuple-element.10.own_hbm, ...), custom_call_target="tpu_custom_call" | custom-call | tf_op jit(solution)/shard_map/far/pallas_call | solution.py:344

commit v6 on v5

--- a/solution.py
+++ b/solution.py
@@ -71,9 +71,8 @@
     step = block.shape[0]
 
     def some(g, carry):
-        rows = rows_ref.at[pl.ds(g * step, step)]
         for u in range(step):
-            block[pl.ds(u, 1), :] = wide[pl.ds(rows[u], 1), :]
+            block[pl.ds(u, 1), :] = wide[pl.ds(rows_ref[u % cap, g * (step // cap) + u // cap], 1), :]
         out_ref[pl.ds(pl.multiple_of(g * step, step), step), :] = block[...].astype(BF16)
         return carry
 
@@ -184,7 +183,7 @@
         functools.partial(exchange_kernel, n_sec, n_sub),
         out_shape=(
             jax.ShapeDtypeStruct((leaf_dev, coeffs), BF16),
-            jax.ShapeDtypeStruct((rows.shape[0], coeffs), BF16),
+            jax.ShapeDtypeStruct((rows.size, coeffs), BF16),
             jax.ShapeDtypeStruct((devices // 2, 2, share, coeffs), BF16),
             jax.ShapeDtypeStruct((leaf_dev, panels), F32),
         ),
@@ -198,7 +197,7 @@
             pltpu.VMEM(near_list.shape, I32),
             pltpu.VMEM((leaf_dev, coeffs), F32),
             pltpu.VMEM((128, coeffs), F32),
-            pltpu.VMEM((rows.shape[0], coeffs), BF16),
+            pltpu.VMEM((rows.size, coeffs), BF16),
             pltpu.VMEM((share, coeffs), BF16),
             pltpu.VMEM((2, 4, EDGE, panels), F32),
             pltpu.VMEM((2, 4, EDGE, panels), F32),
@@ -311,7 +310,7 @@
     for load in loads[5:]:
         load.wait()
     total[...] = jnp.zeros_like(total)
-    chunk = 28
+    chunk = 52
 
     def multiply(first, count):
         left = jnp.concatenate([grouped[first + t] for t in range(count)], axis=1)
@@ -377,8 +376,7 @@
     send_rows, send_counts, leaf_list, leaf_types, parent_list, parent_types, near_list,
 ):
     n_sec, n_sub = lax.axis_size("sec"), lax.axis_size("sub")
-    rows = send_rows.reshape(n_sec * n_sub * send_rows.shape[2])
-    own, arrived, parents, near = exchange(n_sec, n_sub, rows, charges, p2m, m2m, positions, near_list)
+    own, arrived, parents, near = exchange(n_sec, n_sub, send_rows[0].T, charges, p2m, m2m, positions, near_list)
     parents = parents.reshape(parents.shape[0] * parents.shape[1] * parents.shape[2], parents.shape[3])
     return far_field(leaf_list, parent_list, leaf_types, parent_types, arrived, own, parents, m2l, l2l, l2p, near)
 

time: 92.5 us -> 90.8 us (0.982)
  local copies, waits for them, and re-layouts: 1.5 us -> 0 us
where the time goes in v6:
time: 90.8 us; the launch traced here: 90.6 us
  Pallas kernels  90.6 us (100%)
    pallas_call x1, Pallas kernels, far_field(): pl.pallas_call(far_kernel, out_shape=jax.ShapeDtypeStruct(near.shape, F32...  52.2 us
    pallas_call x1, Pallas kernels, exchange(): pl.pallas_call(functools.partial(exchange_kernel, n_sec, n_sub), out_shap...  38.4 us

profile of v6, /device:TPU:1, one launch (start us, length us, event | category | flops | bytes accessed | tf_op | source)
XLA Modules:
  0.0 90.6 jit_solution(18085272970062475399)
XLA Ops:
  0.0 38.4 %exchange.1 = (bf16[256,128]{1,0:T(8,128)(2,1)}, bf16[4096,128]{1,0:T(8,128)(2,1)}, bf16[64,2,32,128]{3,2,1,0:T(8,128)(2,1)}, f32[256,128]{1,0:T(8,128)}) custom-call(s32[32,128]{1,0:T(8,128)} %bitcast.9, bf16[256,128]{1,0:T(8,128)(2,1)} %charge_hbm.1, bf16[128,128]{1,0:T(8,128)(2,1)} %p2m_hbm.1, bf16[8,128,128]{2,1,0:T(8,128)(2,1)} %m2m_hbm.1, ...), custom_call_target="tpu_custom_call" | custom-call | tf_op jit(solution)/shard_map/exchange/pallas_call | solution.py:182
  38.4 52.2 %far.1 = f32[256,128]{1,0:T(8,128)} custom-call(s32[189,256]{1,0:T(8,128)} %bitcast.7, s32[32,189]{1,0:T(8,128)} %parent_list_ref.1, s32[189,256]{1,0:T(8,128)} %bitcast.8, s32[32,189]{1,0:T(8,128)} %parent_types_ref.1, bf16[4096,128]{1,0:T(8,128)(2,1)} %get-tuple-element.9.arrived_hbm, bf16[256,128]{1,0:T(8,128)(2,1)} %get-tuple-element.10.own_hbm, ...), custom_call_target="tpu_custom_call" | custom-call | tf_op jit(solution)/shard_map/far/pallas_call | solution.py:343
